TPU v7x, 128 devices: a whole 4x4x4 slice. The times are simulated.
128 devices in a mesh: row: 16 (over x_hi, y, core), col: 8 (over z, x_lo).
Axes of the slice: x: 4 (x_hi: 2, x_lo: 2; x = x_hi * 2 + x_lo), y: 4, z: 4, core: 2. Of those that a mesh axis runs over, the one named last changes fastest.
Arguments:
- emb_a: bfloat16 [512, 1280], P('row', 'col'), may hold values from -70 to 70
- emb_b: bfloat16 [2048, 1280], P('col', 'row'), may hold values from -8 to 8
- w_query: bfloat16 [1280, 1280], replicated, may hold values from -1 to 1
- w_key: bfloat16 [1280, 1280], replicated, may hold values from -1 to 1
- w_value: bfloat16 [1280, 1280], replicated, may hold values from -0.15625 to 0.15625
- w_out: bfloat16 [1280, 1280], replicated, may hold values from -3 to 3
- w_pair_a: bfloat16 [1280, 64], replicated, may hold values from -0.15625 to 0.15625
- w_pair_b: bfloat16 [1280, 64], replicated, may hold values from -0.15625 to 0.15625
- w_depth: float32 [2, 64, 25], replicated, may hold values from -1.25 to 1.25
- w_point: bfloat16 [2, 64, 64], replicated, may hold values from -0.75 to 0.75
- w_logit: float32 [64], replicated, may hold values from -0.75 to 0.75
Outputs:
- logits: float32 [512, 2048], P('row', 'col')
All inputs are finite; a program needn't handle non-finite values.
Results may differ from a plain program's by a relative error of at most 0.024.
Values may be sent and summed in bfloat16 or wider, within the bound.
A program may use at most 64 MiB of HBM per device.

v0:
```python
import math

import jax
import jax.numpy as jnp
from jax import lax
from jax.sharding import PartitionSpec as P

E = 1280
H = 16


def extended_2(cells, sides, width):
    for axis, dim in sides:
        count = lax.axis_size(axis)
        ends = count - 1
        head = lax.slice_in_dim(cells, 0, width, axis=dim)
        tail = lax.slice_in_dim(cells, cells.shape[dim] - width, cells.shape[dim], axis=dim)
        cells = jnp.concatenate(
            [
                lax.ppermute(tail, axis, [(i, (i + 1) % count) for i in range(ends)]),
                cells,
                lax.ppermute(head, axis, [((i + 1) % count, i) for i in range(ends)]),
            ],
            axis=dim,
        )
    return cells


def combined_all(x, axis, join):
    gathered = jax.tree.map(
        lambda a, kind: lax.all_gather(a.astype(kind), axis),
        x,
        (jnp.bfloat16, jnp.bfloat16, jnp.bfloat16),
    )

    def take(source):
        return jax.tree.map(
            lambda a, own: lax.dynamic_index_in_dim(a, source, 0, False).astype(own.dtype),
            gathered,
            x,
        )

    return lax.fori_loop(
        1, lax.axis_size(axis), lambda source, state: join(state, take(source)), take(0)
    )


def layer_norm(values, axis):
    centre = values - jnp.mean(values, axis, keepdims=True)
    spread = jnp.mean(centre * centre, axis, keepdims=True)
    return centre * lax.rsqrt(spread + 1e-05)


def conv_block(extended, tap_weights, point_weights, count_r, count_c):
    wide = extended.astype(jnp.float32)
    depth = jnp.zeros((wide.shape[0], count_r, count_c), jnp.float32)
    for offset in range(25):
        shift_r, shift_c = divmod(offset, 5)
        depth = (
            depth
            + tap_weights[:, offset][:, None, None]
            * wide[:, shift_r : shift_r + count_r, shift_c : shift_c + count_c]
        )
    normed = jax.nn.gelu(layer_norm(depth, 0)).astype(jnp.bfloat16)
    update = lax.dot_general(
        point_weights, normed, (((0,), (0,)), ((), ())), preferred_element_type=jnp.float32
    )
    result = (wide[:, 2 : 2 + count_r, 2 : 2 + count_c] + update).astype(jnp.bfloat16)
    return result


def narrow_rim(field):
    return extended_2(field, (("row", 1), ("col", 2)), 2)


def outer_sum(rows_part, cols_part):
    return jnp.transpose(rows_part)[:, :, None] + jnp.transpose(cols_part)[:, None, :]


def local(
    emb_a, emb_b, w_query, w_key, w_value, w_out, w_pair_a, w_pair_b, w_depth, w_point, w_logit
):
    head_size = E // H
    feats_a = lax.all_gather(emb_a, "col", axis=1, tiled=True)
    count_a = feats_a.shape[0]
    query = jnp.dot(feats_a, w_query, preferred_element_type=jnp.float32).astype(jnp.bfloat16)
    feats_b = lax.all_gather(emb_b, "row", axis=1, tiled=True)
    key_proj = jnp.dot(feats_b, w_key, preferred_element_type=jnp.float32).astype(jnp.bfloat16)
    value_proj = jnp.dot(feats_b, w_value, preferred_element_type=jnp.float32).astype(jnp.bfloat16)
    pair_b = jnp.dot(feats_b, w_pair_b, preferred_element_type=jnp.float32)
    query_heads = query.reshape(count_a, H, head_size)
    key_heads = key_proj.reshape(-1, H, head_size)
    value_heads = value_proj.reshape(-1, H, head_size)
    scores = jnp.einsum(
        "ihd,jhd->hij", query_heads, key_heads, preferred_element_type=jnp.float32
    ) / math.sqrt(head_size)
    highest = jnp.max(scores, -1)
    weights = jnp.exp(scores - highest[:, :, None])
    totals = jnp.sum(weights, -1)
    partial_sum = jnp.einsum(
        "hij,jhd->ihd",
        weights.astype(jnp.bfloat16),
        value_heads,
        preferred_element_type=jnp.float32,
    ).reshape(count_a, E)

    def combine(first_part, second_part):
        high_one, total_one, accum_one = first_part
        high_two, total_two, accum_two = second_part
        summit = jnp.maximum(high_one, high_two)
        scale_one = jnp.exp(high_one - summit)
        scale_two = jnp.exp(high_two - summit)
        merged = (
            accum_one.reshape(-1, H, head_size) * jnp.transpose(scale_one)[:, :, None]
            + accum_two.reshape(-1, H, head_size) * jnp.transpose(scale_two)[:, :, None]
        )
        return (summit, total_one * scale_one + total_two * scale_two, merged.reshape(-1, E))

    summit, total_all, accum_all = combined_all((highest, totals, partial_sum), "col", combine)
    attended = (
        (accum_all.reshape(count_a, H, head_size) / jnp.transpose(total_all)[:, :, None])
        .reshape(count_a, E)
        .astype(jnp.bfloat16)
    )
    hidden_a = feats_a.astype(jnp.float32) + jnp.dot(
        attended, w_out, preferred_element_type=jnp.float32
    )
    pair_a = jnp.dot(
        layer_norm(hidden_a, -1).astype(jnp.bfloat16), w_pair_a, preferred_element_type=jnp.float32
    )
    count_b = pair_b.shape[0]
    field = outer_sum(pair_a, pair_b).astype(jnp.bfloat16)
    for section_idx in range(2):
        field = conv_block(
            narrow_rim(field), w_depth[section_idx], w_point[section_idx], count_a, count_b
        )
    return jnp.einsum("c,cij->ij", w_logit, field.astype(jnp.float32))


def solution(mesh):
    in_specs = (P("row", "col"), P("col", "row"), P(), P(), P(), P(), P(), P(), P(), P(), P())
    out_specs = P("row", "col")
    return jax.shard_map(local, mesh=mesh, in_specs=in_specs, out_specs=out_specs, check_vma=False)
```

profile of v0, /device:TPU:57, one launch (start us, length us, event | category | flops | bytes accessed | tf_op | source)
XLA Modules:
  0.0 316.6 jit_solution(1108320215910875349)
XLA Ops:
  0.0 21.4 %all-gather.2 = bf16[8,160,32]{1,2,0:T(8,128)(2,1)S(1)} all-gather(bf16[1,160,32]{1,2,0:T(8,128)(2,1)} %bitcast.199), channel_id=1, replica_groups=mesh['row'=16,'col'=8] {'col'}, dimensions={0}, use_global_device_ids=true | all-gather | bytes 92160 | tf_op jit(solution)/shard_map/all_gather | solution.py:84
  21.7 3.3 %convolution_convert_fusion.2 = bf16[32,1280]{1,0:T(8,128)(2,1)} fusion(bf16[1280,32]{0,1:T(8,128)(2,1)S(1)} %reshape.190, bf16[1280,1280]{1,0:T(8,128)(2,1)} %param.15), kind=kOutput, calls=%fused_computation.15 | convolution fusion | flops 104898560 | bytes 3440640 | tf_op jit(solution)/shard_map/dot_general | solution.py:86
  26.0 26.3 %all_gather.19 = bf16[256,1280]{0,1:T(8,128)(2,1)S(1)} all-gather(bf16[256,80]{0,1:T(8,128)(2,1)S(1)} %copy-done.10), channel_id=1, replica_groups=mesh['row'=16,'col'=8] {'row'}, dimensions={1}, use_global_device_ids=true | all-gather | bytes 696320 | tf_op jit(solution)/shard_map/all_gather | solution.py:87
  54.1 1.9 convolution_convert_fusion
  56.1 1.9 convolution_convert_fusion.1
  57.9 2.2 copy.34
  60.1 2.2 copy.36
  64.7 23.4 %all-gather = bf16[128,32]{1,0:T(8,128)(2,1)} all-gather(bf16[16,32]{1,0:T(8,128)(2,1)S(1)} %convert_element_type.147), channel_id=2, replica_groups=mesh['row'=16,'col'=8] {'col'}, dimensions={0}, use_global_device_ids=true | all-gather | bytes 9216 | tf_op jit(solution)/shard_map/all_gather | solution.py:31
  89.4 23.4 %all-gather.1 = bf16[128,32]{1,0:T(8,128)(2,1)} all-gather(bf16[16,32]{1,0:T(8,128)(2,1)S(1)} %fusion.92), channel_id=3, replica_groups=mesh['row'=16,'col'=8] {'col'}, dimensions={0}, use_global_device_ids=true | all-gather | bytes 9216 | tf_op jit(solution)/shard_map/all_gather | solution.py:31
  114.1 24.6 %all_gather.22 = bf16[8,32,1280]{2,1,0:T(8,128)(2,1)S(1)} all-gather(bf16[1,32,1280]{2,1,0:T(8,128)(2,1)S(1)} %convert_element_type.159), channel_id=1, replica_groups=mesh['row'=16,'col'=8] {'col'}, dimensions={0}, use_global_device_ids=true | all-gather | bytes 737280 | tf_op jit(solution)/shard_map/all_gather | solution.py:31
  139.5 54.7 %while.19 = (s32[]{:T(128)}, f32[16,32]{1,0:T(8,128)}, f32[16,32]{1,0:T(8,128)}, f32[32,1280]{1,0:T(8,128)}, bf16[8,16,32]{2,1,0:T(8,128)(2,1)}, /*index=5*/bf16...) while((s32[]{:T(128)}, f32[16,32]{1,0:T(8,128)}, ...), condition=%wide.region_3.4_spmd, body=%wide.region_2.3_spmd.sunk | while | flops 168965 | bytes 1756307 | solution.py:43
  145.5 1.8 fusion.152
  153.3 1.8 fusion.152
  161.1 1.8 fusion.152
  169.0 1.8 fusion.152
  196.0 2.9 fusion.129
  199.7 26.4 %collective-permute-start = (bf16[64,2,256]{2,0,1:T(8,128)(2,1)S(1)}, bf16[64,2,256]{2,0,1:T(8,128)(2,1)S(1)}, u32[]{:S(2)}, u32[]{:S(2)}) collective-permute-start(bf16[64,2,256]{2,0,1:T(8,128)(2,1)S(1)} %get-tuple-element.212), channel_id=1, source_target_pairs={{0,8},{8,16},{16,24},{24,32},{32,40},{40,48},{48,56},{56,64},{64,7... | collective-permute-start | bytes 196616 | tf_op jit(solution)/shard_map/ppermute | solution.py:20
  226.1 1.9 collective-permute-start.1
  228.7 6.6 %collective-permute-done.1 = bf16[64,2,256]{2,0,1:T(8,128)(2,1)S(1)} collective-permute-done((bf16[64,2,256]{2,0,1:T(8,128)(2,1)S(1)}, bf16[64,2,256]{2,0,1:T(8,128)(2,1)S(1)}, u32[]{:S(2)}, u32[]{:S(2)}) %collective-permute-start.1) | collective-permute-done | bytes 65568 | tf_op jit(solution)/shard_map/ppermute | solution.py:22
  239.5 5.4 %collective-permute-start.3 = (bf16[64,36,2]{0,2,1:T(2,128)(2,1)S(1)}, bf16[64,36,2]{0,2,1:T(2,128)(2,1)S(1)}, u32[]{:S(2)}, u32[]{:S(2)}) collective-permute-start(bf16[64,36,2]{0,2,1:T(2,128)(2,1)S(1)} %copy.40), channel_id=1, source_target_pairs={{1,0},{2,1},{3,2},{4,3},{5,4},{6,5},{7,6},{9,8},{10,9},{11,10},{12... | collective-permute-start | bytes 27656 | tf_op jit(solution)/shard_map/ppermute | solution.py:22
  244.9 2.1 collective-permute-start.2
  247.6 2.7 collective-permute-done.2
  252.7 2.5 maximum_convert_fusion
  255.4 11.4 %fusion.121 = (f32[32,256]{1,0:T(8,128)S(1)}, f32[64,32,256]{2,0,1:T(8,128)S(1)}) fusion(f32[64,36,260]{2,0,1:T(8,128)S(1)} %maximum_convert_fusion, f32[64]{0:T(128)S(1)} %get-tuple-element.242, f32[64]{0:T(128)S(1)} %get-tuple-element.243, f32[64]{0:T(128)S(1)} %get-tuple-element.244, f32[64]{0:T(128)S(1)} %get-tuple-element.245, ...), kind=kLoop, calls=%fused_computation.241 | loop fusion | flops 26206208 | bytes 54565120 | tf_op jit(solution)/shard_map/reduce_sum | solution.py:49
  269.1 3.9 %collective-permute-start.4 = (bf16[64,2,256]{2,0,1:T(8,128)(2,1)S(1)}, bf16[64,2,256]{2,0,1:T(8,128)(2,1)S(1)}, u32[]{:S(2)}, u32[]{:S(2)}) collective-permute-start(bf16[64,2,256]{2,0,1:T(8,128)(2,1)S(1)} %get-tuple-element.210), channel_id=1, source_target_pairs={{0,8},{8,16},{16,24},{24,32},{32,40},{40,48},{48,56},{56,64},{64,7... | collective-permute-start | bytes 196616 | tf_op jit(solution)/shard_map/ppermute | solution.py:20
  273.0 1.9 collective-permute-start.5
  275.5 6.6 %collective-permute-done.5 = bf16[64,2,256]{2,0,1:T(8,128)(2,1)S(1)} collective-permute-done((bf16[64,2,256]{2,0,1:T(8,128)(2,1)S(1)}, bf16[64,2,256]{2,0,1:T(8,128)(2,1)S(1)}, u32[]{:S(2)}, u32[]{:S(2)}) %collective-permute-start.5) | collective-permute-done | bytes 65568 | tf_op jit(solution)/shard_map/ppermute | solution.py:22
  286.4 1.9 collective-permute-start.7
  288.3 3.6 %collective-permute-start.6 = (bf16[64,36,2]{0,2,1:T(2,128)(2,1)S(1)}, bf16[64,36,2]{0,2,1:T(2,128)(2,1)S(1)}, u32[]{:S(2)}, u32[]{:S(2)}) collective-permute-start(bf16[64,36,2]{0,2,1:T(2,128)(2,1)S(1)} %copy.45), channel_id=1, source_target_pairs={{0,1},{1,2},{2,3},{3,4},{4,5},{5,6},{6,7},{8,9},{9,10},{10,11},{11... | collective-permute-start | bytes 27656 | tf_op jit(solution)/shard_map/ppermute | solution.py:20
  296.1 2.5 maximum_convert_fusion.1
  298.8 11.4 %fusion.119 = (f32[32,256]{1,0:T(8,128)S(1)}, f32[64,32,256]{2,0,1:T(8,128)S(1)}) fusion(f32[64,36,260]{2,0,1:T(8,128)S(1)} %maximum_convert_fusion.1, f32[64]{0:T(128)S(1)} %get-tuple-element.217, f32[64]{0:T(128)S(1)} %get-tuple-element.218, f32[64]{0:T(128)S(1)} %get-tuple-element.219, f32[64]{0:T(128)S(1)} %get-tuple-element.220, ...), kind=kLoop, calls=%fused_computation.240 | loop fusion | flops 26206208 | bytes 54565120 | tf_op jit(solution)/shard_map/reduce_sum | solution.py:49
  311.9 4.0 %fusion.71 = f32[1,32,256]{2,0,1:T(1,128)S(1)} fusion(f32[64,36,260]{2,0,1:T(8,128)} %copy-done.1, f32[64,32,256]{2,0,1:T(8,128)} %copy-done.3, f32[32,256]{1,0:T(8,128)S(1)} %add_rsqrt_fusion, f32[32,256]{1,0:T(8,128)S(1)} %broadcast_multiply_fusion, bf16[2,64,64]{2,1,0:T(8,128)(2,1)S(1)} %copy-done.44, f32[64]{0:T(128)S(1)} %copy-done.45), kind=kOutput, calls=%fused_computation.137 | convolution fusion | flops 74973184 | bytes 4309504 | tf_op jit(solution)/shard_map/c,cij->ij/dot_general | solution.py:137
  (212 shorter events, 79.9 us)
Async XLA Ops:
  0.0 54.1 %copy-start = (bf16[1280,1280]{1,0:T(8,128)(2,1)S(1)}, bf16[1280,1280]{1,0:T(8,128)(2,1)}, u32[]{:S(2)}) copy-start(bf16[1280,1280]{1,0:T(8,128)(2,1)} %param.17) | copy-start | bytes 9830404
  21.4 4.6 %copy-start.10 = (bf16[256,80]{0,1:T(8,128)(2,1)S(1)}, bf16[256,80]{0,1:T(8,128)(2,1)}, u32[]{:S(2)}) copy-start(bf16[256,80]{0,1:T(8,128)(2,1)} %param.14) | copy-start | bytes 122884
  21.7 30.7 %copy-start.7 = (bf16[1280,32]{0,1:T(8,128)(2,1)}, bf16[1280,32]{0,1:T(8,128)(2,1)S(1)}, u32[]{:S(2)}) copy-start(bf16[1280,32]{0,1:T(8,128)(2,1)S(1)} %reshape.190) | copy-start | bytes 245764
  195.9 3.1 copy-start.9
  195.9 3.3 %copy-start.8 = (f32[64,256]{1,0:T(8,128)S(1)}, f32[64,256]{1,0:T(8,128)}, u32[]{:S(2)}) copy-start(f32[64,256]{1,0:T(8,128)} %fusion.132) | copy-start | bytes 196612
  196.0 32.0 %copy-start.11 = (f32[2,64,25]{1,0,2:T(2,128)S(1)}, f32[2,64,25]{1,0,2:T(2,128)}, u32[]{:S(2)}) copy-start(f32[2,64,25]{1,0,2:T(2,128)} %param.21) | copy-start | bytes 38404
  199.7 37.1 %copy-start.2 = (bf16[64,32,256]{2,0,1:T(8,128)(2,1)}, bf16[64,32,256]{2,0,1:T(8,128)(2,1)S(1)}, u32[]{:S(2)}) copy-start(bf16[64,32,256]{2,0,1:T(8,128)(2,1)S(1)} %add_convert_fusion) | copy-start | bytes 3145732
  199.7 29.0 %collective-permute-start = (bf16[64,2,256]{2,0,1:T(8,128)(2,1)S(1)}, bf16[64,2,256]{2,0,1:T(8,128)(2,1)S(1)}, u32[]{:S(2)}, u32[]{:S(2)}) collective-permute-start(bf16[64,2,256]{2,0,1:T(8,128)(2,1)S(1)} %get-tuple-element.212), channel_id=1, source_target_pairs={{0,8},{8,16},{16,24},{24,32},{32,40},{40,48},{48,56},{56,64},{64,7... | collective-permute-start | bytes 196616 | tf_op jit(solution)/shard_map/ppermute | solution.py:20
  226.1 9.2 %collective-permute-start.1 = (bf16[64,2,256]{2,0,1:T(8,128)(2,1)S(1)}, bf16[64,2,256]{2,0,1:T(8,128)(2,1)S(1)}, u32[]{:S(2)}, u32[]{:S(2)}) collective-permute-start(bf16[64,2,256]{2,0,1:T(8,128)(2,1)S(1)} %get-tuple-element.213), channel_id=1, source_target_pairs={{8,0},{16,8},{24,16},{32,24},{40,32},{48,40},{56,48},{64,56},{72,6... | collective-permute-start | bytes 196616 | tf_op jit(solution)/shard_map/ppermute | solution.py:22
  239.5 12.0 %collective-permute-start.3 = (bf16[64,36,2]{0,2,1:T(2,128)(2,1)S(1)}, bf16[64,36,2]{0,2,1:T(2,128)(2,1)S(1)}, u32[]{:S(2)}, u32[]{:S(2)}) collective-permute-start(bf16[64,36,2]{0,2,1:T(2,128)(2,1)S(1)} %copy.40), channel_id=1, source_target_pairs={{1,0},{2,1},{3,2},{4,3},{5,4},{6,5},{7,6},{9,8},{10,9},{11,10},{12... | collective-permute-start | bytes 27656 | tf_op jit(solution)/shard_map/ppermute | solution.py:22
  244.9 5.4 %collective-permute-start.2 = (bf16[64,36,2]{0,2,1:T(2,128)(2,1)S(1)}, bf16[64,36,2]{0,2,1:T(2,128)(2,1)S(1)}, u32[]{:S(2)}, u32[]{:S(2)}) collective-permute-start(bf16[64,36,2]{0,2,1:T(2,128)(2,1)S(1)} %copy.39), channel_id=1, source_target_pairs={{0,1},{1,2},{2,3},{3,4},{4,5},{5,6},{6,7},{8,9},{9,10},{10,11},{11... | collective-permute-start | bytes 27656 | tf_op jit(solution)/shard_map/ppermute | solution.py:20
  252.6 2.7 copy-start.14
  252.6 2.7 copy-start.15
  252.6 2.7 copy-start.16
  252.6 2.7 copy-start.17
  252.6 2.7 copy-start.18
  252.6 2.7 copy-start.19
  252.6 2.7 copy-start.20
  252.6 2.7 copy-start.21
  252.6 2.7 copy-start.22
  252.7 2.7 copy-start.30
  252.7 2.7 copy-start.31
  252.7 2.7 copy-start.32
  252.7 2.7 copy-start.33
  252.7 2.7 copy-start.34
  252.7 2.7 copy-start.35
  269.0 14.6 %copy-start.4 = (bf16[64,32,256]{2,0,1:T(8,128)(2,1)}, bf16[64,32,256]{2,0,1:T(8,128)(2,1)S(1)}, u32[]{:S(2)}) copy-start(bf16[64,32,256]{2,0,1:T(8,128)(2,1)S(1)} %fusion.70) | copy-start | bytes 3145732
  269.1 6.5 %collective-permute-start.4 = (bf16[64,2,256]{2,0,1:T(8,128)(2,1)S(1)}, bf16[64,2,256]{2,0,1:T(8,128)(2,1)S(1)}, u32[]{:S(2)}, u32[]{:S(2)}) collective-permute-start(bf16[64,2,256]{2,0,1:T(8,128)(2,1)S(1)} %get-tuple-element.210), channel_id=1, source_target_pairs={{0,8},{8,16},{16,24},{24,32},{32,40},{40,48},{48,56},{56,64},{64,7... | collective-permute-start | bytes 196616 | tf_op jit(solution)/shard_map/ppermute | solution.py:20
  273.0 9.2 %collective-permute-start.5 = (bf16[64,2,256]{2,0,1:T(8,128)(2,1)S(1)}, bf16[64,2,256]{2,0,1:T(8,128)(2,1)S(1)}, u32[]{:S(2)}, u32[]{:S(2)}) collective-permute-start(bf16[64,2,256]{2,0,1:T(8,128)(2,1)S(1)} %get-tuple-element.211), channel_id=1, source_target_pairs={{8,0},{16,8},{24,16},{32,24},{40,32},{48,40},{56,48},{64,56},{72,6... | collective-permute-start | bytes 196616 | tf_op jit(solution)/shard_map/ppermute | solution.py:22
  286.4 8.4 %collective-permute-start.7 = (bf16[64,36,2]{0,2,1:T(2,128)(2,1)S(1)}, bf16[64,36,2]{0,2,1:T(2,128)(2,1)S(1)}, u32[]{:S(2)}, u32[]{:S(2)}) collective-permute-start(bf16[64,36,2]{0,2,1:T(2,128)(2,1)S(1)} %copy.46), channel_id=1, source_target_pairs={{1,0},{2,1},{3,2},{4,3},{5,4},{6,5},{7,6},{9,8},{10,9},{11,10},{12... | collective-permute-start | bytes 27656 | tf_op jit(solution)/shard_map/ppermute | solution.py:22
  288.3 5.4 %collective-permute-start.6 = (bf16[64,36,2]{0,2,1:T(2,128)(2,1)S(1)}, bf16[64,36,2]{0,2,1:T(2,128)(2,1)S(1)}, u32[]{:S(2)}, u32[]{:S(2)}) collective-permute-start(bf16[64,36,2]{0,2,1:T(2,128)(2,1)S(1)} %copy.45), channel_id=1, source_target_pairs={{0,1},{1,2},{2,3},{3,4},{4,5},{5,6},{6,7},{8,9},{9,10},{10,11},{11... | collective-permute-start | bytes 27656 | tf_op jit(solution)/shard_map/ppermute | solution.py:20
  298.6 11.6 %copy-start.1 = (f32[64,36,260]{2,0,1:T(8,128)}, f32[64,36,260]{2,0,1:T(8,128)S(1)}, u32[]{:S(2)}) copy-start(f32[64,36,260]{2,0,1:T(8,128)S(1)} %maximum_convert_fusion.1) | copy-start | bytes 7188484
  (22 other events, 50.2 us)
where the time goes:
time: 319 us; the launch traced here: 317 us
  blocking collectives  119 us (37%)
  other arithmetic  60.2 us (19%)
  local copies, waits for them, and re-layouts  52.9 us (17%)
  starting transfers between devices  47.1 us (15%)
  matrix products  19.2 us (6%)
  waiting for transfers between devices  17.1 us (5%)
    all_gather x3, blocking collectives, combined_all(): lax.all_gather(a.astype(kind), axis)  71.4 us
    ppermute x4, starting transfers between devices, extended_2(): lax.ppermute(tail, axis, [(i, (i + 1) % count) for i in range(ends)])  35.9 us
    all_gather x1, blocking collectives, local(): feats_b = lax.all_gather(emb_b, 'row', axis=1, tiled=True)  26.3 us
    reduce_sum x2, other arithmetic, layer_norm(): centre = values - jnp.mean(values, axis, keepdims=True)  22.9 us
    all_gather x1, blocking collectives, local(): feats_a = lax.all_gather(emb_a, 'col', axis=1, tiled=True)  21.4 us
    ppermute x4, waiting for transfers between devices, extended_2(): lax.ppermute(head, axis, [((i + 1) % count, i) for i in range(ends)])  13.2 us
    add x7, other arithmetic, combine(): accum_one.reshape(-1, H, head_size) * jnp.transpose(scale_one)[:, :, None]  12.7 us
    mul x14, local copies, waits for them, and re-layouts, combine(): accum_two.reshape(-1, H, head_size) * jnp.transpose(scale_two)[:, :, None]  11.5 us
  transfers between devices with their start and end apart: 8, of which 4 were waited for; matrix products, arithmetic and copies ran while one was open for 1% of the time, Pallas kernels for 0%

commit v1 on v0

v1 whole, which is shorter than its diff:
```python
import functools
import math

import jax
import jax.numpy as jnp
from jax import lax
from jax.experimental import pallas as pl
from jax.experimental.pallas import tpu as pltpu
from jax.sharding import PartitionSpec as P

E = 1280
H = 16
D = E // H
C = 64
ROWS = 16
COLS = 8
LA = 512
LB = 2048
TILE_A = LA // ROWS
TILE_B = LB // COLS
HALF = TILE_B // 2
F32 = jnp.float32
BF16 = jnp.bfloat16
MESH = pl.DeviceIdType.MESH
NN = (((1,), (0,)), ((), ()))
NT = (((1,), (1,)), ((), ()))


def dot(a, b, dims=NN):
    return lax.dot_general(a, b, dims, preferred_element_type=F32)


def iota(shape, axis):
    return lax.broadcasted_iota(jnp.int32, shape, axis)


def eye(n):
    return jnp.where(iota((n, n), 0) == iota((n, n), 1), 1.0, 0.0).astype(BF16)


def doubled(n):
    lane = iota((n, 2 * n), 1)
    lane = jnp.where(lane >= n, lane - n, lane)
    return jnp.where(iota((n, 2 * n), 0) == lane, 1.0, 0.0).astype(BF16)


def split3(x):
    high = x.astype(BF16)
    rest = x - high.astype(F32)
    mid = rest.astype(BF16)
    low = (rest - mid.astype(F32)).astype(BF16)
    return high, mid, low


def exact_dot(x, ones, dims=NN):
    return sum(dot(part, ones, dims) for part in split3(x))


def attention(
    ea_h, eb_h, wq_h, wk_h, wv_h, wo_h, wpa_h, wpb_h,
    pa_ref, pb_ref,
    ea, wq, wk, wv, wo, wpa, wpb,
    fb_src, fb_all, fa_all, fa_rows, msg, land,
    pb_own, pb_sib, pb_left, pb_right, pa_own, pa_land,
    in_sem, fb_s, fb_r, fa_s, fa_r, rs_s, rs_r, pb_s, pb_r, pa_s, pa_r,
):
    r = lax.axis_index("row")
    c = lax.axis_index("col")
    k = lax.rem(r, 2)
    p = lax.div(r, 2)
    mine = k * COLS + c

    loads = [
        pltpu.make_async_copy(src, dst, in_sem.at[i])
        for i, (src, dst) in enumerate(
            [(eb_h.at[:, pl.ds(0, HALF)], fb_src.at[0]), (eb_h.at[:, pl.ds(HALF, HALF)], fb_src.at[1]),
             (ea_h, ea), (wq_h, wq), (wk_h, wk), (wv_h, wv),
             (wpb_h, wpb), (wo_h, wo), (wpa_h, wpa)]
        )
    ]
    for load in loads:
        load.start()
    w_eb0, w_eb1, w_ea, w_q, w_k, w_v, w_pb, w_o, w_pa = loads

    def group_peer(e):
        g = lax.rem(mine + e, 2 * COLS)
        return 2 * p + lax.div(g, COLS), lax.rem(g, COLS)

    barrier = pltpu.get_barrier_semaphore()

    def greet(row, col):
        pl.semaphore_signal(barrier, inc=1, device_id=(row, col), device_id_type=MESH)

    @pl.loop(1, ROWS)
    def _(d):
        greet(lax.rem(r + d, ROWS), c)
        greet(*group_peer(d))

    @pl.when((k == 1) & (r < ROWS - 1))
    def _():
        greet(r + 1, 0)

    @pl.when((k == 0) & (r > 0))
    def _():
        greet(r - 2, COLS - 1)

    pa_land[...] = jnp.zeros_like(pa_land)
    w_eb0.wait()
    w_eb1.wait()
    fb_all[pl.ds(r, 1)] = fb_src[pl.ds(k, 1)]
    w_ea.wait()
    fa_all[pl.ds(mine, 1)] = ea[...][None]

    first = (k == 0) & (c == 0) & (p > 0)
    last = (k == 0) & (c == COLS - 1) & (p < ROWS // 2 - 1)
    extra = jnp.where(first, COLS, 0) + jnp.where(last, COLS, 0)
    pl.semaphore_wait(barrier, 2 * (ROWS - 1) + extra)

    def fb_copy(d):
        to = lax.rem(r + d, ROWS)
        return pltpu.make_async_remote_copy(
            src_ref=fb_src.at[lax.rem(to, 2)], dst_ref=fb_all.at[r],
            send_sem=fb_s.at[d], recv_sem=fb_r.at[d],
            device_id=(to, c), device_id_type=MESH)

    def fa_copy(e):
        return pltpu.make_async_remote_copy(
            src_ref=ea, dst_ref=fa_all.at[mine],
            send_sem=fa_s.at[e], recv_sem=fa_r.at[e],
            device_id=group_peer(e), device_id_type=MESH)

    @pl.loop(1, ROWS)
    def _(d):
        fb_copy(d).start()
        fa_copy(d).start()

    @pl.loop(1, ROWS)
    def _(d):
        fa_copy(d).wait_recv()

    fa = jnp.concatenate(
        [jnp.concatenate([fa_all[kk * COLS + cc].astype(F32) for cc in range(COLS)], axis=1)
         for kk in range(2)], axis=0)
    fa_rows[...] = fa
    w_q.wait()
    query = dot(fa.astype(BF16), wq[...]).astype(BF16).astype(F32)
    w_pb.wait()
    wpb2 = jnp.concatenate([wpb[...], wpb[...]], axis=0)

    @pl.loop(1, ROWS)
    def _(d):
        fb_copy(d).wait_recv()

    fb = dot(eye(HALF), fb_all[...].reshape(E, HALF), NT).astype(BF16)
    pb_own[...] = dot(fb, wpb2, NT)

    def sib_copy():
        return pltpu.make_async_remote_copy(
            src_ref=pb_own, dst_ref=pb_sib, send_sem=pb_s.at[0], recv_sem=pb_r.at[0],
            device_id=(2 * p + 1 - k, c), device_id_type=MESH)

    def right_copy(kk):
        return pltpu.make_async_remote_copy(
            src_ref=pb_own.at[pl.ds(HALF - 8, 8)], dst_ref=pb_left,
            send_sem=pb_s.at[1 + kk], recv_sem=pb_r.at[1],
            device_id=(2 * p + kk, lax.rem(c + 1, COLS)), device_id_type=MESH)

    def left_copy(kk):
        return pltpu.make_async_remote_copy(
            src_ref=pb_own.at[pl.ds(0, 8)], dst_ref=pb_right,
            send_sem=pb_s.at[1 + kk], recv_sem=pb_r.at[2],
            device_id=(2 * p + kk, lax.rem(c + COLS - 1, COLS)), device_id_type=MESH)

    sends_right = (k == 1) & (c < COLS - 1)
    sends_left = (k == 0) & (c > 0)
    sib_copy().start()

    @pl.when(sends_right)
    def _():
        right_copy(0).start()
        right_copy(1).start()

    @pl.when(sends_left)
    def _():
        left_copy(0).start()
        left_copy(1).start()

    w_k.wait()
    rows = 2 * TILE_A
    scores = [None] * H
    lane256 = iota((rows, 256), 1)
    for t in range(5):
        key_t = dot(fb, wk[:, 256 * t:256 * t + 256]).astype(BF16)
        parts = []
        for h in range(3 * t, 3 * t + 4):
            low, high = D * h - 256 * t, D * h + D - 256 * t
            parts.append(jnp.where((lane256 >= low) & (lane256 < high),
                                   query[:, 256 * t:256 * t + 256], 0.0))
        found = dot(jnp.concatenate(parts, axis=0).astype(BF16), key_t, NT)
        for n, h in enumerate(range(3 * t, 3 * t + 4)):
            piece = found[rows * n:rows * n + rows]
            scores[h] = piece if scores[h] is None else scores[h] + piece

    lane = iota((rows, 128), 1)
    head_of = lane & (H - 1)
    tops = jnp.zeros((rows, 128), F32)
    totals = jnp.zeros((rows, 128), F32)
    weights = []
    for h in range(H):
        s = scores[h] * (1.0 / math.sqrt(D))
        top = jnp.max(s, axis=1, keepdims=True)
        w = jnp.exp(s - top)
        tops = jnp.where(head_of == h, top, tops)
        totals = jnp.where(head_of == h, jnp.sum(w, axis=1, keepdims=True), totals)
        weights.append(w.astype(BF16))
    t1, t2, t3 = (x.astype(F32) for x in split3(tops))
    n1, n2, _ = (x.astype(F32) for x in split3(totals))
    stats = jnp.where(lane < 16, t1, jnp.where(lane < 32, t2, jnp.where(
        lane < 48, t3, jnp.where(lane < 64, n1, jnp.where(lane < 80, n2, 0.0)))))

    w_v.wait()
    mixed = []
    for t in range(5):
        value_t = dot(fb, wv[:, 256 * t:256 * t + 256]).astype(BF16)
        found = dot(jnp.concatenate(weights[3 * t:3 * t + 4], axis=0), value_t)
        total = None
        for n, h in enumerate(range(3 * t, 3 * t + 4)):
            low, high = D * h - 256 * t, D * h + D - 256 * t
            piece = jnp.where((lane256 >= low) & (lane256 < high),
                              found[rows * n:rows * n + rows], 0.0)
            total = piece if total is None else total + piece
        mixed += [total[:, :128], total[:, 128:]]
    for d in range(COLS):
        block = [m[8 * d:8 * d + 8] for m in mixed + [stats]] + [jnp.zeros((8, 128), F32)]
        msg[d] = jnp.concatenate(block, axis=0).astype(BF16)

    def rs_copy(d):
        to = lax.rem(c + d, COLS)
        return pltpu.make_async_remote_copy(
            src_ref=msg.at[to], dst_ref=land.at[mine],
            send_sem=rs_s.at[d], recv_sem=rs_r.at[mine],
            device_id=(2 * p, to), device_id_type=MESH)

    def rs_arrival(g):
        return pltpu.make_async_remote_copy(
            src_ref=msg.at[0], dst_ref=land.at[g],
            send_sem=rs_s.at[0], recv_sem=rs_r.at[g],
            device_id=(2 * p, c), device_id_type=MESH)

    @pl.when(k == 1)
    def _():
        rs_copy(0).start()

    @pl.loop(1, COLS)
    def _(d):
        rs_copy(d).start()

    sib_copy().wait_recv()

    @pl.when(c > 0)
    def _():
        right_copy(0).wait_recv()

    @pl.when(c < COLS - 1)
    def _():
        left_copy(0).wait_recv()

    left_lane = iota((HALF, 128), 1) < C
    left8 = iota((8, 128), 1) < C
    zero8 = jnp.zeros((8, 128), F32)
    own, sib = pb_own[...], pb_sib[...]
    even = k == 0
    block0 = jnp.where(even, own, sib)
    block1 = jnp.where(even, sib, own)
    from_left = jnp.where(c > 0, pb_left[...], zero8)
    from_right = jnp.where(c < COLS - 1, pb_right[...], zero8)
    pb_ref[0:8] = jnp.where(left8, from_left, block0[HALF - 8:])
    pb_ref[8:8 + HALF] = jnp.where(left_lane, block0, block1)
    pb_ref[8 + HALF:16 + HALF] = jnp.where(left8, block1[:8], from_right)

    def pa_copy(row, col, slot, sem):
        return pltpu.make_async_remote_copy(
            src_ref=pa_own, dst_ref=pa_land.at[slot],
            send_sem=pa_s.at[sem], recv_sem=pa_r.at[slot],
            device_id=(row, col), device_id_type=MESH)

    targets = (
        (2 * p, c + 1, c <= 4, 0),
        (2 * p + 1, c - 3, c >= 3, 8),
        (2 * p - 1, 5, (c == 0) & (p > 0), 8),
        (2 * p + 2, 0, (c == COLS - 1) & (p < ROWS // 2 - 1), 0),
    )
    w_o.wait()
    w_pa.wait()

    @pl.when(k == 0)
    def _():
        land[pl.ds(c, 1)] = msg[pl.ds(c, 1)]

        @pl.loop(0, 2 * COLS)
        def _(g):
            @pl.when(g != c)
            def _():
                rs_arrival(g).wait_recv()

        got = [land[g].astype(F32) for g in range(2 * COLS)]
        stat = jnp.concatenate([x[80:88] for x in got], axis=0).astype(BF16)
        a, b = iota((128, 128), 0), iota((128, 128), 1)
        same = (a & (H - 1)) == (b & (H - 1))
        pick_top = jnp.where(same & (a < 48), 1.0, 0.0).astype(BF16)
        pick_total = jnp.where(same & (a >= 48) & (a < 80), 1.0, 0.0).astype(BF16)
        top = dot(stat, pick_top)
        total = dot(stat, pick_total)
        tops = [top[8 * g:8 * g + 8] for g in range(2 * COLS)]
        summit = functools.reduce(jnp.maximum, tops)
        scales = [jnp.exp(x - summit) for x in tops]
        whole = sum(s * total[8 * g:8 * g + 8] for g, s in enumerate(scales))
        factor = jnp.concatenate([s / whole for s in scales], axis=0)
        high = factor.astype(BF16).astype(F32)
        factor = jnp.where(b < H, high, jnp.where(b < 2 * H, factor - high, 0.0)).astype(BF16)
        l, f = iota((128, E), 0), iota((128, E), 1)
        first = (l & (H - 1)) * D
        spread = jnp.where((l < 2 * H) & (f >= first) & (f < first + D), 1.0, 0.0).astype(BF16)
        factors = dot(factor, spread)
        attended = []
        for t in range(10):
            attended.append(sum(
                got[g][8 * t:8 * t + 8] * factors[8 * g:8 * g + 8, 128 * t:128 * t + 128]
                for g in range(2 * COLS)))
        attended = jnp.concatenate(attended, axis=1).astype(BF16)
        hidden = fa_rows[pl.ds(pl.multiple_of(8 * c, 8), 8), :] + dot(attended, wo[...])
        centre = hidden - jnp.mean(hidden, axis=1, keepdims=True)
        spread_h = jnp.mean(centre * centre, axis=1, keepdims=True)
        normed = (centre * lax.rsqrt(spread_h + 1e-5)).astype(BF16)
        pa_own[...] = dot(normed, jnp.concatenate([wpa[...], wpa[...]], axis=0), NT)
        for row, slot, on, base in targets:
            @pl.when(on)
            def _():
                @pl.loop(0, COLS)
                def _(col):
                    local = (row == r) & (col == c)

                    @pl.when(local)
                    def _():
                        pa_land[pl.ds(slot, 1)] = pa_own[...][None]

                    @pl.when(jnp.logical_not(local))
                    def _():
                        pa_copy(row, col, slot, base + col).start()

    mine_slot = jnp.where((k == 0) & (c <= 4), c + 1, -1)

    @pl.loop(0, 6)
    def _(s):
        outside = ((s == 0) & (r == 0)) | ((s == 5) & (r == ROWS - 1))

        @pl.when(jnp.logical_not(outside) & (s != mine_slot))
        def _():
            pa_copy(r, c, s, 0).wait_recv()

    for s in range(6):
        pa_ref[8 * s:8 * s + 8] = pa_land[s]

    @pl.loop(1, ROWS)
    def _(d):
        fb_copy(d).wait_send()
        fa_copy(d).wait_send()

    sib_copy().wait_send()

    @pl.when(sends_right)
    def _():
        right_copy(0).wait_send()
        right_copy(1).wait_send()

    @pl.when(sends_left)
    def _():
        left_copy(0).wait_send()
        left_copy(1).wait_send()

    @pl.when(k == 1)
    def _():
        rs_copy(0).wait_send()

    @pl.loop(1, COLS)
    def _(d):
        rs_copy(d).wait_send()

    @pl.when(k == 0)
    def _():
        for row, slot, on, base in targets:
            @pl.when(on)
            def _():
                @pl.loop(0, COLS)
                def _(col):
                    @pl.when(jnp.logical_not((row == r) & (col == c)))
                    def _():
                        pa_copy(row, col, slot, base + col).wait_send()


def gelu(x):
    inner = x * (0.7978845608028654 + 0.035677408136300125 * (x * x))
    return (0.5 * x) * (1.0 + jnp.tanh(inner))


WIDE = 136


def pair_map(pa_ref, pb_ref, wd_ref, wp_ref, wl_ref, out_ref,
             taps, a_mid, a_edge, b_part, pb_mid, pb_in, f1, logits):
    r = lax.axis_index("row")
    c = lax.axis_index("col")
    a, b = iota((128, 128), 0), iota((128, 128), 1)
    same_half = (a < C) == (b < C)
    mean_of = jnp.where(same_half, 1.0 / C, 0.0).astype(BF16)
    double = doubled(C)

    for s in range(2):
        taps[s] = exact_dot(wd_ref[s], double)
    point = dot(wp_ref[0], double)
    point = jnp.where(same_half, jnp.concatenate([point, point], axis=0), 0.0).astype(BF16)
    read = jnp.broadcast_to(wl_ref[...], (8, C))
    folded = exact_dot(read, wp_ref[1], NT)
    row8, lane8 = iota((8, 128), 0), iota((8, 128), 1)
    half8 = (row8 & 1) == jnp.where(lane8 < C, 0, 1)

    def readout(x):
        both = exact_dot(x, double)
        high = both.astype(BF16).astype(F32)
        picked = jnp.where(row8 < 2, high, jnp.where(row8 < 4, both - high, 0.0))
        return jnp.where(half8, picked, 0.0).astype(BF16)

    heads = jnp.concatenate([readout(read), readout(folded)], axis=1)

    q48 = iota((48, 128), 0) + (TILE_A * r - 8)
    pa = jnp.where((q48 >= 0) & (q48 < LA), pa_ref[...], 0.0)
    q144, l144 = iota((144, 128), 0), iota((144, 128), 1)
    col144 = q144 + TILE_B * c + jnp.where(l144 < C, -4, HALF - 4)
    ok144 = (col144 >= 0) & (col144 < LB) & (q144 < WIDE)
    pb_in[0:140] = pb_ref[4:144]
    pb_in[140:144] = jnp.zeros((4, 128), F32)
    pb = jnp.where(ok144, pb_in[...], 0.0)
    pb_in[...] = pb
    pb_mid[...] = pb_in[2:2 + WIDE]
    ok = jnp.where(ok144, 1.0, 0.0)

    def tap(u, v):
        return taps[0, 5 * u + v:5 * u + v + 1, :]

    def centred(x):
        return x - exact_dot(x, mean_of)

    a_sum = None
    for u in range(5):
        weight = sum(tap(u, v) for v in range(5))
        piece = weight * pa[4 + u:44 + u]
        a_sum = piece if a_sum is None else a_sum + piece
    a_mid[...] = centred(a_sum)
    for n, start in enumerate((0, WIDE - 8)):
        weights = [sum(tap(u, v) * ok[start + v:start + v + 8] for v in range(5)) for u in range(5)]
        for i in range(36):
            value = sum(weights[u] * pa[4 + u + i:5 + u + i] for u in range(5))
            a_edge[n, 8 * i:8 * i + 8] = value
        a_edge[n] = centred(a_edge[n])
    for n, (low, high) in enumerate(((2, 5), (1, 5), (0, 5), (0, 4), (0, 3))):
        value = None
        for v in range(5):
            weight = sum(tap(u, v) for u in range(low, high))
            piece = weight * pb_in[v:v + WIDE]
            value = piece if value is None else value + piece
        b_part[n] = centred(value)

    vv, ll = iota((WIDE, 128), 0), iota((WIDE, 128), 1)
    col_v = vv + TILE_B * c + jnp.where(ll < C, -2, HALF - 2)
    in_map = (col_v >= 0) & (col_v < LB)
    n_first = 4

    @pl.loop(0, 36 // n_first)
    def _(step):
        xs, bases, keeps = [], [], []
        for s in range(n_first):
            u = step * n_first + s
            row = TILE_A * r - 2 + u
            kind = jnp.where(row == 0, 0, jnp.where(row == 1, 1, jnp.where(
                row == LA - 2, 3, jnp.where(row == LA - 1, 4, 2))))
            part = b_part[kind]
            at = pl.multiple_of(8 * u, 8)
            xs += [part[:8] + a_edge[0, pl.ds(at, 8)],
                   part[8:128] + a_mid[pl.ds(u, 1)],
                   part[128:] + a_edge[1, pl.ds(at, 8)]]
            bases.append(pb_mid[...] + pa_ref[pl.ds(u + 6, 1)])
            keeps.append(in_map & (row >= 0) & (row < LA))
        x = jnp.concatenate(xs, axis=0)
        var = dot((x * x).astype(BF16), mean_of)
        g = gelu(x * lax.rsqrt(var + 1e-5)).astype(BF16)
        update = dot(g, point)
        for s in range(n_first):
            u = step * n_first + s
            field = bases[s] + update[WIDE * s:WIDE * s + WIDE]
            field = jnp.where(keeps[s], field, 0.0).astype(BF16).astype(F32)
            f1[u] = field

    n_second = 4

    @pl.loop(0, TILE_A // n_second)
    def _(step):
        depths, fields = [], []
        for s in range(n_second):
            i = step * n_second + s
            total = None
            for u in range(5):
                for v in range(5):
                    piece = taps[1, 5 * u + v:5 * u + v + 1, :] * f1[i + u, v:v + HALF, :]
                    total = piece if total is None else total + piece
            depths.append(total)
            fields.append(f1[i + 2, 2:2 + HALF, :].astype(BF16))
        depth = jnp.concatenate(depths, axis=0)
        high = depth.astype(BF16)
        low = (depth - high.astype(F32)).astype(BF16)
        x = depth - (dot(high, mean_of) + dot(low, mean_of))
        var = dot((x * x).astype(BF16), mean_of)
        g = gelu(x * lax.rsqrt(var + 1e-5)).astype(BF16)
        both = jnp.concatenate([jnp.concatenate(fields, axis=0), g], axis=1)
        found = dot(heads, both, NT)
        left = found[0:1] + found[2:3]
        right = found[1:2] + found[3:4]
        for s in range(n_second):
            i = step * n_second + s
            logits[pl.ds(i, 1)] = left[:, HALF * s:HALF * s + HALF]
            logits[pl.ds(TILE_A + i, 1)] = right[:, HALF * s:HALF * s + HALF]

    out_ref[:, 0:HALF] = logits[0:TILE_A]
    out_ref[:, HALF:TILE_B] = logits[TILE_A:2 * TILE_A]


def local(
    emb_a, emb_b, w_query, w_key, w_value, w_out, w_pair_a, w_pair_b, w_depth, w_point, w_logit
):
    hbm = pl.BlockSpec(memory_space=pl.ANY)
    vmem = pl.BlockSpec(memory_space=pltpu.VMEM)
    weight = pltpu.VMEM((E, E), BF16)
    dma = pltpu.SemaphoreType.DMA
    pair_a, pair_b = pl.pallas_call(
        attention,
        out_shape=(jax.ShapeDtypeStruct((48, 128), F32), jax.ShapeDtypeStruct((144, 128), F32)),
        in_specs=[hbm] * 8,
        out_specs=(vmem, vmem),
        scratch_shapes=[
            pltpu.VMEM((TILE_A, E // COLS), BF16),
            weight, weight, weight, weight,
            pltpu.VMEM((C, E), BF16),
            pltpu.VMEM((C, E), BF16),
            pltpu.VMEM((2, D, HALF), BF16),
            pltpu.VMEM((ROWS, D, HALF), BF16),
            pltpu.VMEM((2 * COLS, TILE_A, E // COLS), BF16),
            pltpu.VMEM((2 * TILE_A, E), F32),
            pltpu.VMEM((COLS, 96, 128), BF16),
            pltpu.VMEM((2 * COLS, 96, 128), BF16),
            pltpu.VMEM((HALF, 128), F32),
            pltpu.VMEM((HALF, 128), F32),
            pltpu.VMEM((8, 128), F32),
            pltpu.VMEM((8, 128), F32),
            pltpu.VMEM((8, 128), F32),
            pltpu.VMEM((6, 8, 128), F32),
            dma((9,)),
            dma((16,)), dma((16,)),
            dma((16,)), dma((16,)),
            dma((8,)), dma((16,)),
            dma((3,)), dma((3,)),
            dma((16,)), dma((6,)),
        ],
        compiler_params=pltpu.CompilerParams(
            collective_id=0, has_side_effects=True, vmem_limit_bytes=60 * 2 ** 20),
        name="attention",
    )(emb_a, emb_b.T, w_query, w_key, w_value, w_out, w_pair_a.T, w_pair_b.T)
    return pl.pallas_call(
        pair_map,
        out_shape=jax.ShapeDtypeStruct((TILE_A, TILE_B), F32),
        in_specs=[vmem] * 5,
        out_specs=vmem,
        scratch_shapes=[
            pltpu.VMEM((2, 25, 128), F32),
            pltpu.VMEM((40, 128), F32),
            pltpu.VMEM((2, 288, 128), F32),
            pltpu.VMEM((5, WIDE, 128), F32),
            pltpu.VMEM((WIDE, 128), F32),
            pltpu.VMEM((144, 128), F32),
            pltpu.VMEM((36, WIDE, 128), F32),
            pltpu.VMEM((2 * TILE_A, 128), F32),
        ],
        compiler_params=pltpu.CompilerParams(vmem_limit_bytes=32 * 2 ** 20),
        name="pair_map",
    )(pair_a, pair_b, jnp.swapaxes(w_depth, 1, 2), w_point, w_logit.reshape(1, C))


def solution(mesh):
    in_specs = (P("row", "col"), P("col", "row"), P(), P(), P(), P(), P(), P(), P(), P(), P())
    out_specs = P("row", "col")
    return jax.shard_map(local, mesh=mesh, in_specs=in_specs, out_specs=out_specs, check_vma=False)
```

time: 319 us -> 50 us (0.16)
  the two profiles are of different devices: /device:TPU:57 before, /device:TPU:6 now
where the time goes in v1:
time: 50 us; the launch traced here: 49.7 us
  Pallas kernels  47.3 us (95%)
  local copies, waits for them, and re-layouts  2.36 us (5%)
    pallas_call x1, Pallas kernels, local(): pl.pallas_call(attention, out_shape=(jax.ShapeDtypeStruct((48, 128), F32)...  34.2 us
    pallas_call x1, Pallas kernels, local(): pl.pallas_call(pair_map, out_shape=jax.ShapeDtypeStruct((TILE_A, TILE_B),...  13.1 us
    unnamed x9, local copies, waits for them, and re-layouts  2.36 us

profile of v1, /device:TPU:6, one launch (start us, length us, event | category | flops | bytes accessed | tf_op | source)
XLA Modules:
  0.0 49.7 jit_solution(8384574119411500877)
XLA Ops:
  0.0 0.7 %copy.14 = f32[2,64,25]{1,2,0:T(8,128)S(1)} copy(f32[2,64,25]{1,0,2:T(2,128)} %param.19) | data formatting | bytes 25600 | tf_op args[8]
  0.7 0.0 copy-start.1
  0.7 0.0 copy-start.3
  0.7 34.2 %attention.1 = (f32[48,128]{1,0:T(8,128)}, f32[144,128]{1,0:T(8,128)}) custom-call(bf16[32,160]{1,0:T(8,128)(2,1)} %ea_h.1, bf16[80,256]{1,0:T(8,128)(2,1)} %bitcast.11, bf16[1280,1280]{1,0:T(8,128)(2,1)} %wq_h.1, bf16[1280,1280]{1,0:T(8,128)(2,1)} %wk_h.1, bf16[1280,1280]{1,0:T(8,128)(2,1)} %wv_h.1, bf16[1280,1280]{1,0:T(8,128)(2,1)} %wo_h.1, ...), custom_call_target="tpu_custom_call" | custom-call | tf_op jit(solution)/shard_map/attention/pallas_call | solution.py:543
  35.0 0.0 copy-done.1
  35.0 0.0 copy-done.3
  35.0 0.0 copy-start
  35.0 0.9 %copy-done = f32[144,128]{1,0:T(8,128)S(1)} copy-done((f32[144,128]{1,0:T(8,128)S(1)}, f32[144,128]{1,0:T(8,128)}, u32[]{:S(2)}) %copy-start) | copy-done | bytes 73752
  35.9 0.0 copy-start.2
  35.9 0.7 %copy-done.2 = f32[48,128]{1,0:T(8,128)S(1)} copy-done((f32[48,128]{1,0:T(8,128)S(1)}, f32[48,128]{1,0:T(8,128)}, u32[]{:S(2)}) %copy-start.2) | copy-done | bytes 24600
  36.6 13.1 %pair_map.1 = f32[32,256]{1,0:T(8,128)} custom-call(f32[48,128]{1,0:T(8,128)S(1)} %copy-done.2, f32[144,128]{1,0:T(8,128)S(1)} %copy-done, f32[2,25,64]{2,1,0:T(8,128)S(1)} %bitcast.7, bf16[2,64,64]{2,1,0:T(8,128)(2,1)S(1)} %copy-done.1, f32[1,64]{1,0:T(1,128)S(1)} %bitcast.8), custom_call_target="tpu_custom_call" | custom-call | tf_op jit(solution)/shard_map/pair_map/pallas_call | solution.py:576
Async XLA Ops:
  0.7 34.2 %copy-start.1 = (bf16[2,64,64]{2,1,0:T(8,128)(2,1)S(1)}, bf16[2,64,64]{2,1,0:T(8,128)(2,1)}, u32[]{:S(2)}) copy-start(bf16[2,64,64]{2,1,0:T(8,128)(2,1)} %wp_ref.1) | copy-start | bytes 49156
  0.7 34.2 %copy-start.3 = (f32[64]{0:T(128)S(1)}, f32[64]{0:T(128)}, u32[]{:S(2)}) copy-start(f32[64]{0:T(128)} %param.21) | copy-start | bytes 772
  35.0 0.9 %copy-start = (f32[144,128]{1,0:T(8,128)S(1)}, f32[144,128]{1,0:T(8,128)}, u32[]{:S(2)}) copy-start(f32[144,128]{1,0:T(8,128)} %get-tuple-element.8.pb_ref) | copy-start | bytes 221188
  35.9 0.7 %copy-start.2 = (f32[48,128]{1,0:T(8,128)S(1)}, f32[48,128]{1,0:T(8,128)}, u32[]{:S(2)}) copy-start(f32[48,128]{1,0:T(8,128)} %get-tuple-element.7.pa_ref) | copy-start | bytes 73732

commit v2 on v1

v2 whole, which is shorter than its diff:
```python
import functools
import math

import jax
import jax.numpy as jnp
from jax import lax
from jax.experimental import pallas as pl
from jax.experimental.pallas import tpu as pltpu
from jax.sharding import PartitionSpec as P

E = 1280
H = 16
D = E // H
C = 64
ROWS = 16
COLS = 8
LA = 512
LB = 2048
TILE_A = LA // ROWS
TILE_B = LB // COLS
HALF = TILE_B // 2
F32 = jnp.float32
BF16 = jnp.bfloat16
MESH = pl.DeviceIdType.MESH
NN = (((1,), (0,)), ((), ()))
NT = (((1,), (1,)), ((), ()))


def dot(a, b, dims=NN):
    return lax.dot_general(a, b, dims, preferred_element_type=F32)


def iota(shape, axis):
    return lax.broadcasted_iota(jnp.int32, shape, axis)


def eye(n):
    return jnp.where(iota((n, n), 0) == iota((n, n), 1), 1.0, 0.0).astype(BF16)


def doubled(n):
    lane = iota((n, 2 * n), 1)
    lane = jnp.where(lane >= n, lane - n, lane)
    return jnp.where(iota((n, 2 * n), 0) == lane, 1.0, 0.0).astype(BF16)


def split3(x):
    high = x.astype(BF16)
    rest = x - high.astype(F32)
    mid = rest.astype(BF16)
    low = (rest - mid.astype(F32)).astype(BF16)
    return high, mid, low


def exact_dot(x, ones, dims=NN):
    return sum(dot(part, ones, dims) for part in split3(x))


QW = 136


def prepare_weights(wd, wp, wl, taps, row_w, edge_w, conv_w, point_w, head_w, c):
    double = doubled(C)
    for s in range(2):
        taps[s, 0:25] = exact_dot(wd[:, s, :], double)

    def tap(u, v):
        return taps[0, 5 * u + v:5 * u + v + 1, :]

    for u in range(5):
        row_w[u:u + 1] = sum(tap(u, v) for v in range(5))
    for n, start in enumerate((0, QW - 8)):
        column = 2 * (iota((8, 128), 0) + start) + jnp.where(iota((8, 128), 1) < C, 0, 1)
        column = column + TILE_B * c - 2
        for u in range(5):
            total = None
            for v in range(5):
                at = column + (v - 2)
                piece = jnp.where((at >= 0) & (at < LB), tap(u, v), 0.0)
                total = piece if total is None else total + piece
            edge_w[n, u] = total

    a, b = iota((128, 128), 0), iota((128, 128), 1)
    upper, left = a < C, b < C
    same = upper == left
    rest = jnp.where((a & (C - 1)) == (b & (C - 1)), 1.0 - 1.0 / C, -1.0 / C)
    columns = sum(dot(jnp.concatenate([eye(C), eye(C)], axis=0), part, NT)
                  for part in split3(wd[:, 1, :]))

    def spread(u, v):
        if not 0 <= v < 5:
            return 0.0
        return columns[:, 5 * u + v:5 * u + v + 1]

    zero = jnp.zeros((128, 128), BF16)
    for q in range(3):
        blocks = []
        for u in range(5):
            block = jnp.where(same, spread(u, 2 * q),
                              jnp.where(upper, spread(u, 2 * q - 1), spread(u, 2 * q + 1)))
            blocks.append((block * rest).astype(BF16))
        for u in range(6):
            at = 128 * (3 * u + q)
            conv_w[at:at + 128, 0:128] = blocks[u] if u < 5 else zero
            conv_w[at:at + 128, 128:256] = blocks[u - 1] if u > 0 else zero

    point = dot(wp[0], double)
    point = jnp.concatenate([point, point], axis=1)
    point = jnp.concatenate([point] * 4, axis=0)
    fits = (iota((256, 256), 0) // C) == (iota((256, 256), 1) // C)
    point_w[...] = jnp.where(fits, 0.5 * point, 0.0).astype(BF16)

    read = jnp.broadcast_to(wl[...], (8, C))
    folded = 0.5 * sum(dot(part, wp[1], NT) for part in split3(read))
    row8, lane8 = iota((8, 256), 0), iota((8, 256), 1)
    fits8 = (row8 & 3) == (lane8 // C)
    for n, values in enumerate((read, folded)):
        both = exact_dot(values, double)
        both = jnp.concatenate([both, both], axis=1)
        high = both.astype(BF16).astype(F32)
        picked = jnp.where(row8 < 4, high, both - high)
        head_w[:, 256 * n:256 * n + 256] = jnp.where(fits8, picked, 0.0).astype(BF16)


def mean_matrix(n):
    fits = (iota((n, n), 0) // C) == (iota((n, n), 1) // C)
    return jnp.where(fits, 1.0 / C, 0.0).astype(BF16)


def column_part(pb_buf, taps, pb_mid, b_part):
    mean = mean_matrix(128)
    left = iota((1, 128), 1) < C
    plain = [pb_buf[6 + q:6 + q + QW] for q in range(3)]
    pb_mid[...] = plain[1]
    crossed = [pltpu.roll(x, C, 1) for x in plain]

    for n, (low, high) in enumerate(((2, 5), (1, 5), (0, 5), (0, 4), (0, 3))):
        w = [sum(taps[0, 5 * u + v:5 * u + v + 1, :] for u in range(low, high)) for v in range(5)]
        value = (w[0] * plain[0] + w[2] * plain[1] + w[4] * plain[2]
                 + jnp.where(left, w[1], 0.0) * crossed[0]
                 + jnp.where(left, w[3], w[1]) * crossed[1]
                 + jnp.where(left, 0.0, w[3]) * crossed[2])
        b_part[n] = value - exact_dot(value, mean)


def attention(
    ea_h, eb_h, wq_h, wk_h, wv_h, wo_h, wpa_h, wpb_h, wd_h, wp_h, wl_h,
    out_ref,
    pa_buf, pb_mid, b_part, row_w, edge_w, conv_w, point_w, head_w, a_mid, a_edge, f1, logits,
    ea, wq, wk, wv, wo, wpa, wpb, wd, wp, wl,
    fb_src, fb_all, fa_all, fa_rows, msg, land,
    pb_own, pb_sib, pb_left, pb_right, pb_buf, pa_own, pa_land, taps,
    in_sem, fb_s, fb_r, fa_s, fa_r, rs_s, rs_r, pb_s, pb_r, pa_s, pa_r,
):
    r = lax.axis_index("row")
    c = lax.axis_index("col")
    k = lax.rem(r, 2)
    p = lax.div(r, 2)
    mine = k * COLS + c

    loads = [
        pltpu.make_async_copy(src, dst, in_sem.at[i])
        for i, (src, dst) in enumerate(
            [(eb_h.at[:, pl.ds(0, HALF)], fb_src.at[0]), (eb_h.at[:, pl.ds(HALF, HALF)], fb_src.at[1]),
             (ea_h, ea), (wq_h, wq), (wk_h, wk), (wv_h, wv),
             (wpb_h, wpb), (wo_h, wo), (wpa_h, wpa), (wd_h, wd), (wp_h, wp), (wl_h, wl)]
        )
    ]
    for load in loads:
        load.start()
    w_eb0, w_eb1, w_ea, w_q, w_k, w_v, w_pb, w_o, w_pa, w_d, w_p, w_l = loads

    x, y = lax.div(r, 8), lax.rem(p, 4)
    z, xl = lax.div(c, 2), lax.rem(c, 2)

    def row_peer(e):
        return (lax.rem(x + lax.div(e, 8), 2) * 8 + lax.rem(y + lax.rem(lax.div(e, 2), 4), 4) * 2
                + lax.rem(k + lax.rem(e, 2), 2))

    def col_peer(e):
        return lax.rem(z + lax.rem(lax.div(e, 2), 4), 4) * 2 + lax.rem(xl + lax.rem(e, 2), 2)

    barrier = pltpu.get_barrier_semaphore()

    def greet(row, col):
        pl.semaphore_signal(barrier, inc=1, device_id=(row, col), device_id_type=MESH)

    @pl.loop(1, ROWS)
    def _(n):
        e = ROWS - n
        greet(row_peer(e), c)
        greet(2 * p + lax.rem(k + lax.div(e, 8), 2), col_peer(e))

    @pl.when((k == 1) & (r < ROWS - 1))
    def _():
        greet(r + 1, 0)

    @pl.when((k == 0) & (r > 0))
    def _():
        greet(r - 2, COLS - 1)

    w_eb0.wait()
    w_eb1.wait()
    fb_all[pl.ds(r, 1)] = fb_src[pl.ds(k, 1)]
    w_ea.wait()
    fa_all[pl.ds(k, 1), pl.ds(c, 1)] = ea[...][None, None]

    first = (k == 0) & (c == 0) & (p > 0)
    last = (k == 0) & (c == COLS - 1) & (p < ROWS // 2 - 1)
    extra = jnp.where(first, COLS, 0) + jnp.where(last, COLS, 0)
    pl.semaphore_wait(barrier, 2 * (ROWS - 1) + extra)

    def fb_copy(e):
        to = row_peer(e)
        return pltpu.make_async_remote_copy(
            src_ref=fb_src.at[lax.rem(to, 2)], dst_ref=fb_all.at[r],
            send_sem=fb_s, recv_sem=fb_r,
            device_id=(to, c), device_id_type=MESH)

    def fb_whole():
        return pltpu.make_async_remote_copy(
            src_ref=fb_all.at[pl.ds(0, ROWS - 1)], dst_ref=fb_all.at[pl.ds(0, ROWS - 1)],
            send_sem=fb_s, recv_sem=fb_r, device_id=(2 * p + 1 - k, c), device_id_type=MESH)

    def fa_whole():
        part = fa_all.at[0, pl.ds(0, COLS - 1)]
        return pltpu.make_async_remote_copy(
            src_ref=part, dst_ref=part, send_sem=fa_s.at[1], recv_sem=fa_r.at[1],
            device_id=(2 * p + 1 - k, c), device_id_type=MESH)

    def fa_copy(e):
        return pltpu.make_async_remote_copy(
            src_ref=ea, dst_ref=fa_all.at[k, c],
            send_sem=fa_s.at[1], recv_sem=fa_r.at[1],
            device_id=(r, col_peer(e)), device_id_type=MESH)

    def fa_sibling():
        return pltpu.make_async_remote_copy(
            src_ref=fa_all.at[k], dst_ref=fa_all.at[k],
            send_sem=fa_s.at[0], recv_sem=fa_r.at[0],
            device_id=(2 * p + 1 - k, c), device_id_type=MESH)

    @pl.loop(1, ROWS)
    def _(n):
        fb_copy(ROWS - n).start()

    @pl.loop(1, COLS)
    def _(n):
        fa_copy(COLS - n).start()

    w_d.wait()
    w_p.wait()
    w_l.wait()
    prepare_weights(wd, wp, wl, taps, row_w, edge_w, conv_w, point_w, head_w, c)

    fa_whole().wait_recv()
    fa_sibling().start()
    fa_sibling().wait_recv()
    fa = jnp.concatenate(
        [jnp.concatenate([fa_all[kk, cc].astype(F32) for cc in range(COLS)], axis=1)
         for kk in range(2)], axis=0)
    fa_rows[...] = fa
    w_q.wait()
    query = dot(fa.astype(BF16), wq[...]).astype(BF16).astype(F32)
    w_pb.wait()
    wpb2 = jnp.concatenate([wpb[...], wpb[...]], axis=0)

    fb_whole().wait_recv()
    n0, n1 = iota((HALF, HALF), 0), iota((HALF, HALF), 1)
    order = jnp.where(n0 < HALF // 2, 2 * n0, 2 * n0 - (HALF - 1))
    order = jnp.where(n1 == order, 1.0, 0.0).astype(BF16)
    fb = dot(order, fb_all[...].reshape(E, HALF), NT).astype(BF16)
    found_b = dot(fb, wpb2, NT)
    pb_own[...] = jnp.where(iota((HALF // 2, 128), 1) < C, found_b[:HALF // 2], found_b[HALF // 2:])

    def sib_copy():
        return pltpu.make_async_remote_copy(
            src_ref=pb_own, dst_ref=pb_sib, send_sem=pb_s.at[0], recv_sem=pb_r.at[0],
            device_id=(2 * p + 1 - k, c), device_id_type=MESH)

    def right_copy(kk):
        return pltpu.make_async_remote_copy(
            src_ref=pb_own.at[pl.ds(HALF // 2 - 8, 8)], dst_ref=pb_left,
            send_sem=pb_s.at[1 + kk], recv_sem=pb_r.at[1],
            device_id=(2 * p + kk, lax.rem(c + 1, COLS)), device_id_type=MESH)

    def left_copy(kk):
        return pltpu.make_async_remote_copy(
            src_ref=pb_own.at[pl.ds(0, 8)], dst_ref=pb_right,
            send_sem=pb_s.at[1 + kk], recv_sem=pb_r.at[2],
            device_id=(2 * p + kk, lax.rem(c + COLS - 1, COLS)), device_id_type=MESH)

    sends_right = (k == 1) & (c < COLS - 1)
    sends_left = (k == 0) & (c > 0)
    sib_copy().start()

    @pl.when(sends_right)
    def _():
        right_copy(0).start()
        right_copy(1).start()

    @pl.when(sends_left)
    def _():
        left_copy(0).start()
        left_copy(1).start()

    w_k.wait()
    rows = 2 * TILE_A
    scores = [None] * H
    lane256 = iota((rows, 256), 1)
    for t in range(5):
        key_t = dot(fb, wk[:, 256 * t:256 * t + 256]).astype(BF16)
        parts = []
        for h in range(3 * t, 3 * t + 4):
            low, high = D * h - 256 * t, D * h + D - 256 * t
            parts.append(jnp.where((lane256 >= low) & (lane256 < high),
                                   query[:, 256 * t:256 * t + 256], 0.0))
        found = dot(jnp.concatenate(parts, axis=0).astype(BF16), key_t, NT)
        for n, h in enumerate(range(3 * t, 3 * t + 4)):
            piece = found[rows * n:rows * n + rows]
            scores[h] = piece if scores[h] is None else scores[h] + piece

    lane = iota((rows, 128), 1)
    head_of = lane & (H - 1)
    tops = jnp.zeros((rows, 128), F32)
    totals = jnp.zeros((rows, 128), F32)
    weights = []
    for h in range(H):
        s = scores[h] * (1.0 / math.sqrt(D))
        top = jnp.max(s, axis=1, keepdims=True)
        w = jnp.exp(s - top)
        tops = jnp.where(head_of == h, top, tops)
        totals = jnp.where(head_of == h, jnp.sum(w, axis=1, keepdims=True), totals)
        weights.append(w.astype(BF16))
    t1, t2, t3 = (x.astype(F32) for x in split3(tops))
    n1, n2, _ = (x.astype(F32) for x in split3(totals))
    stats = jnp.where(lane < 16, t1, jnp.where(lane < 32, t2, jnp.where(
        lane < 48, t3, jnp.where(lane < 64, n1, jnp.where(lane < 80, n2, 0.0)))))

    w_v.wait()
    mixed = []
    for t in range(5):
        value_t = dot(fb, wv[:, 256 * t:256 * t + 256]).astype(BF16)
        found = dot(jnp.concatenate(weights[3 * t:3 * t + 4], axis=0), value_t)
        total = None
        for n, h in enumerate(range(3 * t, 3 * t + 4)):
            low, high = D * h - 256 * t, D * h + D - 256 * t
            piece = jnp.where((lane256 >= low) & (lane256 < high),
                              found[rows * n:rows * n + rows], 0.0)
            total = piece if total is None else total + piece
        mixed += [total[:, :128], total[:, 128:]]
    for d in range(COLS):
        block = [m[8 * d:8 * d + 8] for m in mixed + [stats]] + [jnp.zeros((8, 128), F32)]
        msg[d] = jnp.concatenate(block, axis=0).astype(BF16)

    def rs_copy(d):
        to = col_peer(d)
        return pltpu.make_async_remote_copy(
            src_ref=msg.at[to], dst_ref=land.at[mine],
            send_sem=rs_s, recv_sem=rs_r,
            device_id=(2 * p, to), device_id_type=MESH)

    def rs_whole(n):
        return pltpu.make_async_remote_copy(
            src_ref=land.at[pl.ds(0, n)], dst_ref=land.at[pl.ds(0, n)],
            send_sem=rs_s, recv_sem=rs_r, device_id=(2 * p + 1 - k, c), device_id_type=MESH)

    @pl.loop(1, COLS)
    def _(n):
        rs_copy(COLS - n).start()

    @pl.when(k == 1)
    def _():
        rs_copy(0).start()

    sib_copy().wait_recv()

    @pl.when(c > 0)
    def _():
        right_copy(0).wait_recv()

    @pl.when(c < COLS - 1)
    def _():
        left_copy(0).wait_recv()

    zero8 = jnp.zeros((8, 128), F32)
    own, sib = pb_own[...], pb_sib[...]
    even = k == 0
    pb_buf[0:8] = jnp.where(c > 0, pb_left[...], zero8)
    pb_buf[8:72] = jnp.where(even, own, sib)
    pb_buf[72:136] = jnp.where(even, sib, own)
    pb_buf[136:144] = jnp.where(c < COLS - 1, pb_right[...], zero8)
    pb_buf[144:152] = zero8
    column_part(pb_buf, taps, pb_mid, b_part)

    def pa_copy(row, col, slot, sem):
        return pltpu.make_async_remote_copy(
            src_ref=pa_own, dst_ref=pa_land.at[slot],
            send_sem=pa_s.at[sem], recv_sem=pa_r.at[slot],
            device_id=(row, col), device_id_type=MESH)

    def pa_whole(n, sem):
        part = pb_buf.at[pl.ds(0, 8 * n)]
        return pltpu.make_async_remote_copy(
            src_ref=part, dst_ref=part, send_sem=pa_s.at[sem], recv_sem=pa_r.at[0],
            device_id=(2 * p + 1 - k, c), device_id_type=MESH)

    targets = (
        (2 * p - 1, 5, (c == 0) & (p > 0)),
        (2 * p + 2, 0, (c == COLS - 1) & (p < ROWS // 2 - 1)),
        (2 * p, c + 1, c <= 4),
        (2 * p + 1, c - 3, c >= 3),
    )
    w_o.wait()
    w_pa.wait()

    @pl.when(k == 0)
    def _():
        land[pl.ds(c, 1)] = msg[pl.ds(c, 1)]

        rs_whole(2 * COLS - 1).wait_recv()
        got = [land[g].astype(F32) for g in range(2 * COLS)]
        stat = jnp.concatenate([x[80:88] for x in got], axis=0).astype(BF16)
        a, b = iota((128, 128), 0), iota((128, 128), 1)
        same = (a & (H - 1)) == (b & (H - 1))
        pick_top = jnp.where(same & (a < 48), 1.0, 0.0).astype(BF16)
        pick_total = jnp.where(same & (a >= 48) & (a < 80), 1.0, 0.0).astype(BF16)
        top = dot(stat, pick_top)
        total = dot(stat, pick_total)
        tops = [top[8 * g:8 * g + 8] for g in range(2 * COLS)]
        summit = functools.reduce(jnp.maximum, tops)
        scales = [jnp.exp(x - summit) for x in tops]
        whole = sum(s * total[8 * g:8 * g + 8] for g, s in enumerate(scales))
        factor = jnp.concatenate([s / whole for s in scales], axis=0)
        high = factor.astype(BF16).astype(F32)
        factor = jnp.where(b < H, high, jnp.where(b < 2 * H, factor - high, 0.0)).astype(BF16)
        l, f = iota((128, E), 0), iota((128, E), 1)
        first = (l & (H - 1)) * D
        spread = jnp.where((l < 2 * H) & (f >= first) & (f < first + D), 1.0, 0.0).astype(BF16)
        factors = dot(factor, spread)
        attended = []
        for t in range(10):
            attended.append(sum(
                got[g][8 * t:8 * t + 8] * factors[8 * g:8 * g + 8, 128 * t:128 * t + 128]
                for g in range(2 * COLS)))
        attended = jnp.concatenate(attended, axis=1).astype(BF16)
        hidden = fa_rows[pl.ds(pl.multiple_of(8 * c, 8), 8), :] + dot(attended, wo[...])
        centre = hidden - jnp.mean(hidden, axis=1, keepdims=True)
        spread_h = jnp.mean(centre * centre, axis=1, keepdims=True)
        normed = (centre * lax.rsqrt(spread_h + 1e-5)).astype(BF16)
        pa_own[...] = dot(normed, jnp.concatenate([wpa[...], wpa[...]], axis=0), NT)
        for n, (row, slot, on) in enumerate(targets):
            @pl.when(on)
            def _():
                @pl.loop(0, COLS)
                def _(m):
                    col = col_peer(COLS - 1 - m)
                    local = (row == r) & (col == c)

                    @pl.when(local)
                    def _():
                        pa_land[pl.ds(slot, 1)] = pa_own[...][None]

                    @pl.when(jnp.logical_not(local))
                    def _():
                        pa_copy(row, col, slot, n).start()

    fb_whole().wait_send()
    fa_whole().wait_send()
    fa_sibling().wait_send()
    sib_copy().wait_send()

    @pl.when(sends_right)
    def _():
        right_copy(0).wait_send()
        right_copy(1).wait_send()

    @pl.when(sends_left)
    def _():
        left_copy(0).wait_send()
        left_copy(1).wait_send()

    @pl.when(k == 0)
    def _():
        rs_whole(COLS - 1).wait_send()

    @pl.when(k == 1)
    def _():
        rs_whole(COLS).wait_send()

    mean = mean_matrix(256)
    qq = iota((QW, 128), 0)
    in_map = ((qq > 0) | (c > 0)) & ((qq < HALF + 1) | (c < COLS - 1))
    first = functools.partial(
        first_block, r=r, in_map=in_map, mean=mean, pa_buf=pa_buf, pb_mid=pb_mid, b_part=b_part,
        a_mid=a_mid, a_edge=a_edge, point_w=point_w, f1=f1)
    second = functools.partial(
        second_block, mean=mean, conv_w=conv_w, head_w=head_w, f1=f1, logits=logits)
    mine_slot = jnp.where((k == 0) & (c <= 4), c + 1, -1)
    pa_buf[...] = jnp.zeros_like(pa_buf)
    for s in range(1, 5):
        @pl.when(s != mine_slot)
        def _():
            pa_copy(r, c, s, 0).wait_recv()

        pa_buf[8 * s:8 * s + 8] = pa_land[s]
    row_parts(pa_buf, row_w, edge_w, a_mid, a_edge, 4, 32, r)
    for u in range(4, 32, 2):
        first(u)
    second(1)
    second(2)

    @pl.when(r > 0)
    def _():
        pa_copy(r, c, 0, 0).wait_recv()
        pa_buf[0:8] = pa_land[0]

    @pl.when((r < ROWS - 1) & (mine_slot != 5))
    def _():
        pa_copy(r, c, 5, 0).wait_recv()

    @pl.when(r < ROWS - 1)
    def _():
        pa_buf[40:48] = pa_land[5]

    row_parts(pa_buf, row_w, edge_w, a_mid, a_edge, 0, 4, r)
    row_parts(pa_buf, row_w, edge_w, a_mid, a_edge, 32, 36, r)
    for u in (0, 2, 32, 34):
        first(u)
    second(0)
    second(3)
    out_ref[...] = side_by_side(logits)

    @pl.when(k == 0)
    def _():
        for n, (row, slot, on) in enumerate(targets):
            @pl.when(on & (row == r))
            def _():
                pa_whole(COLS - 1, n).wait_send()

            @pl.when(on & (row != r))
            def _():
                pa_whole(COLS, n).wait_send()


def gelu_twice(x):
    inner = x * (0.7978845608028654 + 0.035677408136300125 * (x * x))
    return x + x * jnp.tanh(inner)


def row_parts(pa_buf, row_w, edge_w, a_mid, a_edge, low, high, r):
    mean = mean_matrix(128)
    place = iota((48, 128), 0) + (TILE_A * r - 8)
    pa = jnp.where((place >= 0) & (place < LA), pa_buf[...], 0.0)
    middle = sum(row_w[u:u + 1] * pa[4 + u:44 + u] for u in range(5))
    weights = [[edge_w[n, u] for u in range(5)] for n in range(2)]
    edges = [sum(weights[n][u] * pa[4 + u + i:5 + u + i] for u in range(5))
             for n in range(2) for i in range(low, high)]
    value = jnp.concatenate([middle] + edges, axis=0)
    value = value - exact_dot(value, mean)
    at = 8 * (high - low)
    a_mid[low:high] = value[low:high]
    a_edge[0, 8 * low:8 * high] = value[40:40 + at]
    a_edge[1, 8 * low:8 * high] = value[40 + at:40 + 2 * at]


def first_block(u, r, in_map, mean, pa_buf, pb_mid, b_part, a_mid, a_edge, point_w, f1):
    top, bottom = r == 0, r == ROWS - 1
    kinds = {2: jnp.where(top, 0, 2), 3: jnp.where(top, 1, 2),
             32: jnp.where(bottom, 3, 2), 33: jnp.where(bottom, 4, 2)}

    def first_part(w):
        part = b_part[kinds.get(w, 2)]
        return jnp.concatenate([
            part[:8] + a_edge[0, 8 * w:8 * w + 8],
            part[8:128] + a_mid[w:w + 1],
            part[128:] + a_edge[1, 8 * w:8 * w + 8]], axis=0)

    x = jnp.concatenate([first_part(u), first_part(u + 1)], axis=1)
    var = dot((x * x).astype(BF16), mean)
    g = gelu_twice(x * lax.rsqrt(var + 1e-5)).astype(BF16)
    update = dot(g, point_w[...])
    for n in range(2):
        keep = in_map
        if u < 2:
            keep = keep & jnp.logical_not(top)
        if u >= 34:
            keep = keep & jnp.logical_not(bottom)
        field = pb_mid[...] + pa_buf[u + n + 6:u + n + 7] + update[:, 128 * n:128 * n + 128]
        f1[u + n] = jnp.where(keep, field, 0.0)


def second_block(step, mean, conv_w, head_w, f1, logits):
    pieces = {}
    for u in range(8 * step, 8 * step + 12):
        for q in range(3):
            pieces[u, q] = f1[u, q:q + HALF, :].astype(BF16)
    cols = []
    for u in range(6):
        for q in range(3):
            cols.append(jnp.concatenate(
                [pieces[8 * step + 2 * n + u, q] for n in range(4)], axis=0))
    x = dot(jnp.concatenate(cols, axis=1), conv_w[...])
    var = dot((x * x).astype(BF16), mean)
    g = gelu_twice(x * lax.rsqrt(var + 1e-5)).astype(BF16)
    both = jnp.concatenate([
        jnp.concatenate([pieces[8 * step + 2 * n + 2, 1] for n in range(4)], axis=0),
        jnp.concatenate([pieces[8 * step + 2 * n + 3, 1] for n in range(4)], axis=0), g], axis=1)
    found = dot(head_w[...], both, NT)
    found = found[0:4] + found[4:8]
    for n in range(4):
        for o in range(2):
            for s in range(2):
                at = TILE_A * s + 8 * step + 2 * n + o
                logits[at:at + 1] = found[2 * o + s:2 * o + s + 1, HALF * n:HALF * n + HALF]


def side_by_side(logits):
    total = None
    for s in range(2):
        place = iota((HALF, TILE_B), 1) == 2 * iota((HALF, TILE_B), 0) + s
        place = jnp.where(place, 1.0, 0.0).astype(BF16)
        piece = exact_dot(logits[TILE_A * s:TILE_A * s + TILE_A], place)
        total = piece if total is None else total + piece
    return total


def local(
    emb_a, emb_b, w_query, w_key, w_value, w_out, w_pair_a, w_pair_b, w_depth, w_point, w_logit
):
    hbm = pl.BlockSpec(memory_space=pltpu.HBM)
    vmem = pl.BlockSpec(memory_space=pltpu.VMEM)
    weight = pltpu.VMEM((E, E), BF16)
    dma = pltpu.SemaphoreType.DMA
    return pl.pallas_call(
        attention,
        out_shape=jax.ShapeDtypeStruct((TILE_A, TILE_B), F32),
        in_specs=[hbm] * 11,
        out_specs=vmem,
        scratch_shapes=[
            pltpu.VMEM((48, 128), F32),
            pltpu.VMEM((QW, 128), F32),
            pltpu.VMEM((5, QW, 128), F32),
            pltpu.VMEM((8, 128), F32),
            pltpu.VMEM((2, 5, 8, 128), F32),
            pltpu.VMEM((18 * 128, 256), BF16),
            pltpu.VMEM((256, 256), BF16),
            pltpu.VMEM((8, 512), BF16),
            pltpu.VMEM((40, 128), F32),
            pltpu.VMEM((2, 288, 128), F32),
            pltpu.VMEM((36, QW, 128), F32),
            pltpu.VMEM((2 * TILE_A, 128), F32),
            pltpu.VMEM((TILE_A, E // COLS), BF16),
            weight, weight, weight, weight,
            pltpu.VMEM((C, E), BF16),
            pltpu.VMEM((C, E), BF16),
            pltpu.VMEM((25, 2, C), F32),
            pltpu.VMEM((2, C, C), BF16),
            pltpu.VMEM((1, C), F32),
            pltpu.VMEM((2, D, HALF), BF16),
            pltpu.VMEM((ROWS, D, HALF), BF16),
            pltpu.VMEM((2, COLS, TILE_A, E // COLS), BF16),
            pltpu.VMEM((2 * TILE_A, E), F32),
            pltpu.VMEM((COLS, 96, 128), BF16),
            pltpu.VMEM((2 * COLS, 96, 128), BF16),
            pltpu.VMEM((HALF // 2, 128), F32),
            pltpu.VMEM((HALF // 2, 128), F32),
            pltpu.VMEM((8, 128), F32),
            pltpu.VMEM((8, 128), F32),
            pltpu.VMEM((152, 128), F32),
            pltpu.VMEM((8, 128), F32),
            pltpu.VMEM((6, 8, 128), F32),
            pltpu.VMEM((2, 32, 128), F32),
            dma((12,)),
            dma, dma,
            dma((2,)), dma((2,)),
            dma, dma,
            dma((3,)), dma((3,)),
            dma((4,)), dma((6,)),
        ],
        compiler_params=pltpu.CompilerParams(
            collective_id=0, has_side_effects=True, vmem_limit_bytes=60 * 2 ** 20),
        name="contact_map",
    )(emb_a, emb_b.T, w_query, w_key, w_value, w_out, w_pair_a.T, w_pair_b.T,
      jnp.transpose(w_depth, (2, 0, 1)), w_point, w_logit.reshape(1, C))


def solution(mesh):
    in_specs = (P("row", "col"), P("col", "row"), P(), P(), P(), P(), P(), P(), P(), P(), P())
    out_specs = P("row", "col")
    return jax.shard_map(local, mesh=mesh, in_specs=in_specs, out_specs=out_specs, check_vma=False)
```

time: 50 us -> 43.5 us (0.87)
  the two profiles are of different devices: /device:TPU:6 before, /device:TPU:1 now
where the time goes in v2:
time: 43.5 us; the launch traced here: 43.4 us
  Pallas kernels  42 us (97%)
  local copies, waits for them, and re-layouts  1.38 us (3%)
    pallas_call x1, Pallas kernels, local(): pl.pallas_call(attention, out_shape=jax.ShapeDtypeStruct((TILE_A, TILE_B)...  42 us
    unnamed x1, local copies, waits for them, and re-layouts  1.38 us

profile of v2, /device:TPU:1, one launch (start us, length us, event | category | flops | bytes accessed | tf_op | source)
XLA Modules:
  0.0 43.4 jit_solution(12845828153463548394)
XLA Ops:
  0.0 42.0 %contact_map.1 = f32[32,256]{1,0:T(8,128)} custom-call(bf16[32,160]{1,0:T(8,128)(2,1)} %ea_h.1, bf16[80,256]{1,0:T(8,128)(2,1)} %bitcast.7, bf16[1280,1280]{1,0:T(8,128)(2,1)} %wq_h.1, bf16[1280,1280]{1,0:T(8,128)(2,1)} %wk_h.1, bf16[1280,1280]{1,0:T(8,128)(2,1)} %wv_h.1, bf16[1280,1280]{1,0:T(8,128)(2,1)} %wo_h.1, bf16[64,1280]{1,0:T(8,128)(2,1)} %bitcast.5, ...), custom_call_target="tpu_custom_call" | custom-call | tf_op jit(solution)/shard_map/contact_map/pallas_call | solution.py:635
  42.0 1.4 %copy.13 = f32[32,256]{1,0:T(8,128)} copy(f32[32,256]{1,0:T(8,128)} %contact_map.1) | data formatting | bytes 65536

commit v3 on v2

--- a/solution.py
+++ b/solution.py
@@ -56,6 +56,11 @@
     return sum(dot(part, ones, dims) for part in split3(x))
 
 
+def near_dot(x, ones):
+    high, mid, _ = split3(x)
+    return dot(high, ones) + dot(mid, ones)
+
+
 QW = 136
 
 
@@ -140,7 +145,7 @@
                  + jnp.where(left, w[1], 0.0) * crossed[0]
                  + jnp.where(left, w[3], w[1]) * crossed[1]
                  + jnp.where(left, 0.0, w[3]) * crossed[2])
-        b_part[n] = value - exact_dot(value, mean)
+        b_part[n] = value - near_dot(value, mean)
 
 
 def attention(
@@ -240,13 +245,13 @@
             send_sem=fa_s.at[0], recv_sem=fa_r.at[0],
             device_id=(2 * p + 1 - k, c), device_id_type=MESH)
 
+    @pl.loop(1, COLS)
+    def _(n):
+        fa_copy(COLS - n).start()
+
     @pl.loop(1, ROWS)
     def _(n):
         fb_copy(ROWS - n).start()
-
-    @pl.loop(1, COLS)
-    def _(n):
-        fa_copy(COLS - n).start()
 
     w_d.wait()
     w_p.wait()
@@ -492,10 +497,10 @@
     qq = iota((QW, 128), 0)
     in_map = ((qq > 0) | (c > 0)) & ((qq < HALF + 1) | (c < COLS - 1))
     first = functools.partial(
-        first_block, r=r, in_map=in_map, mean=mean, pa_buf=pa_buf, pb_mid=pb_mid, b_part=b_part,
+        first_blocks, r=r, in_map=in_map, mean=mean, pa_buf=pa_buf, pb_mid=pb_mid, b_part=b_part,
         a_mid=a_mid, a_edge=a_edge, point_w=point_w, f1=f1)
-    second = functools.partial(
-        second_block, mean=mean, conv_w=conv_w, head_w=head_w, f1=f1, logits=logits)
+    second = functools.partial(correlate, conv_w=conv_w, f1=f1)
+    last_part = functools.partial(read_out, mean=mean, head_w=head_w, logits=logits)
     mine_slot = jnp.where((k == 0) & (c <= 4), c + 1, -1)
     pa_buf[...] = jnp.zeros_like(pa_buf)
     for s in range(1, 5):
@@ -504,11 +509,13 @@
             pa_copy(r, c, s, 0).wait_recv()
 
         pa_buf[8 * s:8 * s + 8] = pa_land[s]
-    row_parts(pa_buf, row_w, edge_w, a_mid, a_edge, 4, 32, r)
-    for u in range(4, 32, 2):
-        first(u)
-    second(1)
-    second(2)
+    row_parts(pa_buf, row_w, edge_w, a_mid, a_edge, range(4, 32), r)
+    for _ in first(list(range(4, 32, 2))):
+        pass
+    part1 = second(1)
+    part2 = second(2)
+    last_part(1, *part1)
+    last_part(2, *part2)
 
     @pl.when(r > 0)
     def _():
@@ -523,12 +530,13 @@
     def _():
         pa_buf[40:48] = pa_land[5]
 
-    row_parts(pa_buf, row_w, edge_w, a_mid, a_edge, 0, 4, r)
-    row_parts(pa_buf, row_w, edge_w, a_mid, a_edge, 32, 36, r)
-    for u in (0, 2, 32, 34):
-        first(u)
-    second(0)
-    second(3)
+    row_parts(pa_buf, row_w, edge_w, a_mid, a_edge, (0, 1, 2, 3, 32, 33, 34, 35), r)
+    for _ in first([0, 2, 32, 34]):
+        pass
+    part0 = second(0)
+    part3 = second(3)
+    last_part(0, *part0)
+    last_part(3, *part3)
     out_ref[...] = side_by_side(logits)
 
     @pl.when(k == 0)
@@ -548,65 +556,80 @@
     return x + x * jnp.tanh(inner)
 
 
-def row_parts(pa_buf, row_w, edge_w, a_mid, a_edge, low, high, r):
-    mean = mean_matrix(128)
+def row_parts(pa_buf, row_w, edge_w, a_mid, a_edge, rows, r):
     place = iota((48, 128), 0) + (TILE_A * r - 8)
     pa = jnp.where((place >= 0) & (place < LA), pa_buf[...], 0.0)
     middle = sum(row_w[u:u + 1] * pa[4 + u:44 + u] for u in range(5))
     weights = [[edge_w[n, u] for u in range(5)] for n in range(2)]
     edges = [sum(weights[n][u] * pa[4 + u + i:5 + u + i] for u in range(5))
-             for n in range(2) for i in range(low, high)]
+             for n in range(2) for i in rows]
     value = jnp.concatenate([middle] + edges, axis=0)
-    value = value - exact_dot(value, mean)
-    at = 8 * (high - low)
-    a_mid[low:high] = value[low:high]
-    a_edge[0, 8 * low:8 * high] = value[40:40 + at]
-    a_edge[1, 8 * low:8 * high] = value[40 + at:40 + 2 * at]
-
-
-def first_block(u, r, in_map, mean, pa_buf, pb_mid, b_part, a_mid, a_edge, point_w, f1):
+    value = value - near_dot(value, mean_matrix(128))
+    for m, i in enumerate(rows):
+        a_mid[i:i + 1] = value[i:i + 1]
+        a_edge[0, 8 * i:8 * i + 8] = value[40 + 8 * m:48 + 8 * m]
+        at = 40 + 8 * (len(rows) + m)
+        a_edge[1, 8 * i:8 * i + 8] = value[at:at + 8]
+
+
+def first_blocks(rows, r, in_map, mean, pa_buf, pb_mid, b_part, a_mid, a_edge, point_w, f1):
     top, bottom = r == 0, r == ROWS - 1
     kinds = {2: jnp.where(top, 0, 2), 3: jnp.where(top, 1, 2),
              32: jnp.where(bottom, 3, 2), 33: jnp.where(bottom, 4, 2)}
 
-    def first_part(w):
+    def part_of(w):
         part = b_part[kinds.get(w, 2)]
         return jnp.concatenate([
             part[:8] + a_edge[0, 8 * w:8 * w + 8],
             part[8:128] + a_mid[w:w + 1],
             part[128:] + a_edge[1, 8 * w:8 * w + 8]], axis=0)
 
-    x = jnp.concatenate([first_part(u), first_part(u + 1)], axis=1)
-    var = dot((x * x).astype(BF16), mean)
-    g = gelu_twice(x * lax.rsqrt(var + 1e-5)).astype(BF16)
-    update = dot(g, point_w[...])
-    for n in range(2):
-        keep = in_map
-        if u < 2:
-            keep = keep & jnp.logical_not(top)
-        if u >= 34:
-            keep = keep & jnp.logical_not(bottom)
-        field = pb_mid[...] + pa_buf[u + n + 6:u + n + 7] + update[:, 128 * n:128 * n + 128]
-        f1[u + n] = jnp.where(keep, field, 0.0)
-
-
-def second_block(step, mean, conv_w, head_w, f1, logits):
+    def start(u):
+        x = jnp.concatenate([part_of(u), part_of(u + 1)], axis=1)
+        return x, dot((x * x).astype(BF16), mean)
+
+    def middle(x, var):
+        return dot(gelu_twice(x * lax.rsqrt(var + 1e-5)).astype(BF16), point_w[...])
+
+    def end(u, update):
+        for n in range(2):
+            keep = in_map
+            if u < 2:
+                keep = keep & jnp.logical_not(top)
+            if u >= 34:
+                keep = keep & jnp.logical_not(bottom)
+            field = pb_mid[...] + pa_buf[u + n + 6:u + n + 7] + update[:, 128 * n:128 * n + 128]
+            f1[u + n] = jnp.where(keep, field, 0.0)
+
+    started, updates = {}, {}
+    count = len(rows)
+    for n in range(count + 2):
+        if n < count:
+            started[n] = start(rows[n])
+        if 1 <= n <= count:
+            updates[n - 1] = middle(*started.pop(n - 1))
+        if n >= 2:
+            end(rows[n - 2], updates.pop(n - 2))
+            yield rows[n - 2]
+
+
+def correlate(step, conv_w, f1):
     pieces = {}
     for u in range(8 * step, 8 * step + 12):
         for q in range(3):
             pieces[u, q] = f1[u, q:q + HALF, :].astype(BF16)
-    cols = []
-    for u in range(6):
-        for q in range(3):
-            cols.append(jnp.concatenate(
-                [pieces[8 * step + 2 * n + u, q] for n in range(4)], axis=0))
-    x = dot(jnp.concatenate(cols, axis=1), conv_w[...])
+
+    def tall(u, q):
+        return jnp.concatenate([pieces[8 * step + 2 * n + u, q] for n in range(4)], axis=0)
+
+    around = jnp.concatenate([tall(u, q) for u in range(6) for q in range(3)], axis=1)
+    return dot(around, conv_w[...]), [tall(2, 1), tall(3, 1)]
+
+
+def read_out(step, x, field, mean, head_w, logits):
     var = dot((x * x).astype(BF16), mean)
     g = gelu_twice(x * lax.rsqrt(var + 1e-5)).astype(BF16)
-    both = jnp.concatenate([
-        jnp.concatenate([pieces[8 * step + 2 * n + 2, 1] for n in range(4)], axis=0),
-        jnp.concatenate([pieces[8 * step + 2 * n + 3, 1] for n in range(4)], axis=0), g], axis=1)
-    found = dot(head_w[...], both, NT)
+    found = dot(head_w[...], jnp.concatenate(field + [g], axis=1), NT)
     found = found[0:4] + found[4:8]
     for n in range(4):
         for o in range(2):
@@ -620,7 +643,7 @@
     for s in range(2):
         place = iota((HALF, TILE_B), 1) == 2 * iota((HALF, TILE_B), 0) + s
         place = jnp.where(place, 1.0, 0.0).astype(BF16)
-        piece = exact_dot(logits[TILE_A * s:TILE_A * s + TILE_A], place)
+        piece = near_dot(logits[TILE_A * s:TILE_A * s + TILE_A], place)
         total = piece if total is None else total + piece
     return total
 

time: 43.5 us -> 38.8 us (0.89)
  Pallas kernels: 42 us -> 37.2 us
    pallas_call x1, Pallas kernels: 42 us -> 37.2 us  [local(): pl.pallas_call(attention, out_shape=jax.ShapeDtypeStruct((TILE_A, TILE_B)...]
where the time goes in v3:
time: 38.8 us; the launch traced here: 38.6 us
  Pallas kernels  37.2 us (96%)
  local copies, waits for them, and re-layouts  1.38 us (4%)
    pallas_call x1, Pallas kernels, local(): pl.pallas_call(attention, out_shape=jax.ShapeDtypeStruct((TILE_A, TILE_B)...  37.2 us
    unnamed x1, local copies, waits for them, and re-layouts  1.38 us

profile of v3, /device:TPU:1, one launch (start us, length us, event | category | flops | bytes accessed | tf_op | source)
XLA Modules:
  0.0 38.6 jit_solution(14713433352123781885)
XLA Ops:
  0.0 37.2 %contact_map.1 = f32[32,256]{1,0:T(8,128)} custom-call(bf16[32,160]{1,0:T(8,128)(2,1)} %ea_h.1, bf16[80,256]{1,0:T(8,128)(2,1)} %bitcast.7, bf16[1280,1280]{1,0:T(8,128)(2,1)} %wq_h.1, bf16[1280,1280]{1,0:T(8,128)(2,1)} %wk_h.1, bf16[1280,1280]{1,0:T(8,128)(2,1)} %wv_h.1, bf16[1280,1280]{1,0:T(8,128)(2,1)} %wo_h.1, bf16[64,1280]{1,0:T(8,128)(2,1)} %bitcast.5, ...), custom_call_target="tpu_custom_call" | custom-call | tf_op jit(solution)/shard_map/contact_map/pallas_call | solution.py:658
  37.3 1.4 %copy.13 = f32[32,256]{1,0:T(8,128)} copy(f32[32,256]{1,0:T(8,128)} %contact_map.1) | data formatting | bytes 65536

commit v4 on v3

--- a/solution.py
+++ b/solution.py
@@ -153,7 +153,7 @@
     out_ref,
     pa_buf, pb_mid, b_part, row_w, edge_w, conv_w, point_w, head_w, a_mid, a_edge, f1, logits,
     ea, wq, wk, wv, wo, wpa, wpb, wd, wp, wl,
-    fb_src, fb_all, fa_all, fa_rows, msg, land,
+    fb_src, fb_all, fa_all, fa_rows, keys, values, spread, msg, land,
     pb_own, pb_sib, pb_left, pb_right, pb_buf, pa_own, pa_land, taps,
     in_sem, fb_s, fb_r, fa_s, fa_r, rs_s, rs_r, pb_s, pb_r, pa_s, pa_r,
 ):
@@ -219,13 +219,14 @@
         to = row_peer(e)
         return pltpu.make_async_remote_copy(
             src_ref=fb_src.at[lax.rem(to, 2)], dst_ref=fb_all.at[r],
-            send_sem=fb_s, recv_sem=fb_r,
+            send_sem=fb_s, recv_sem=fb_r.at[lax.div(e, 8)],
             device_id=(to, c), device_id_type=MESH)
 
-    def fb_whole():
-        return pltpu.make_async_remote_copy(
-            src_ref=fb_all.at[pl.ds(0, ROWS - 1)], dst_ref=fb_all.at[pl.ds(0, ROWS - 1)],
-            send_sem=fb_s, recv_sem=fb_r, device_id=(2 * p + 1 - k, c), device_id_type=MESH)
+    def fb_some(n, far):
+        part = fb_all.at[pl.ds(0, n)]
+        return pltpu.make_async_remote_copy(
+            src_ref=part, dst_ref=part, send_sem=fb_s, recv_sem=fb_r.at[far],
+            device_id=(2 * p + 1 - k, c), device_id_type=MESH)
 
     def fa_whole():
         part = fa_all.at[0, pl.ds(0, COLS - 1)]
@@ -257,9 +258,39 @@
     w_p.wait()
     w_l.wait()
     prepare_weights(wd, wp, wl, taps, row_w, edge_w, conv_w, point_w, head_w, c)
+    l, f = iota((128, E), 0), iota((128, E), 1)
+    start = (l & (H - 1)) * D
+    spread[...] = jnp.where((l < 2 * H) & (f >= start) & (f < start + D), 1.0, 0.0).astype(BF16)
 
     fa_whole().wait_recv()
     fa_sibling().start()
+
+    n0, n1 = iota((HALF, HALF), 0), iota((HALF, HALF), 1)
+    order = jnp.where(n0 < HALF // 2, 2 * n0, 2 * n0 - (HALF - 1))
+    order = jnp.where(n1 == order, 1.0, 0.0).astype(BF16)
+
+    def features(side):
+        blocks = fb_all[pl.ds(8 * side, 8)].reshape(E // 2, HALF)
+        return dot(order, blocks, NT).astype(BF16)
+
+    def some_rows(side):
+        return pl.ds(pl.multiple_of(side * (E // 2), 128), E // 2)
+
+    def pair_weights(side):
+        part = wpb[:, some_rows(side)]
+        return jnp.concatenate([part, part], axis=0)
+
+    fb_some(7, 0).wait_recv()
+    w_k.wait()
+    w_v.wait()
+    w_pb.wait()
+    near = features(x)
+    for t in range(5):
+        at = slice(256 * t, 256 * t + 256)
+        keys[:, at] = dot(near, wk[some_rows(x), at])
+        values[:, at] = dot(near, wv[some_rows(x), at])
+    near_b = dot(near, pair_weights(x), NT)
+
     fa_sibling().wait_recv()
     fa = jnp.concatenate(
         [jnp.concatenate([fa_all[kk, cc].astype(F32) for cc in range(COLS)], axis=1)
@@ -267,15 +298,10 @@
     fa_rows[...] = fa
     w_q.wait()
     query = dot(fa.astype(BF16), wq[...]).astype(BF16).astype(F32)
-    w_pb.wait()
-    wpb2 = jnp.concatenate([wpb[...], wpb[...]], axis=0)
-
-    fb_whole().wait_recv()
-    n0, n1 = iota((HALF, HALF), 0), iota((HALF, HALF), 1)
-    order = jnp.where(n0 < HALF // 2, 2 * n0, 2 * n0 - (HALF - 1))
-    order = jnp.where(n1 == order, 1.0, 0.0).astype(BF16)
-    fb = dot(order, fb_all[...].reshape(E, HALF), NT).astype(BF16)
-    found_b = dot(fb, wpb2, NT)
+
+    fb_some(8, 1).wait_recv()
+    far = features(1 - x)
+    found_b = near_b + dot(far, pair_weights(1 - x), NT)
     pb_own[...] = jnp.where(iota((HALF // 2, 128), 1) < C, found_b[:HALF // 2], found_b[HALF // 2:])
 
     def sib_copy():
@@ -309,20 +335,25 @@
         left_copy(0).start()
         left_copy(1).start()
 
-    w_k.wait()
     rows = 2 * TILE_A
+    lane256 = iota((rows, 256), 1)
+
+    def heads_of(t):
+        return range(3 * t, 3 * t + 4)
+
+    def inside(h, t):
+        return (lane256 >= D * h - 256 * t) & (lane256 < D * h + D - 256 * t)
+
+    spans = [slice(256 * t, 256 * t + 256) for t in range(5)]
+    masked = [jnp.concatenate([jnp.where(inside(h, t), query[:, spans[t]], 0.0)
+                               for h in heads_of(t)], axis=0).astype(BF16) for t in range(5)]
+    key_parts = [keys[:, at] + dot(far, wk[some_rows(1 - x), at]) for at in spans]
+    founds = [dot(masked[t], key_parts[t].astype(BF16), NT) for t in range(5)]
+    value_parts = [values[:, at] + dot(far, wv[some_rows(1 - x), at]) for at in spans]
     scores = [None] * H
-    lane256 = iota((rows, 256), 1)
     for t in range(5):
-        key_t = dot(fb, wk[:, 256 * t:256 * t + 256]).astype(BF16)
-        parts = []
-        for h in range(3 * t, 3 * t + 4):
-            low, high = D * h - 256 * t, D * h + D - 256 * t
-            parts.append(jnp.where((lane256 >= low) & (lane256 < high),
-                                   query[:, 256 * t:256 * t + 256], 0.0))
-        found = dot(jnp.concatenate(parts, axis=0).astype(BF16), key_t, NT)
-        for n, h in enumerate(range(3 * t, 3 * t + 4)):
-            piece = found[rows * n:rows * n + rows]
+        for n, h in enumerate(heads_of(t)):
+            piece = founds[t][rows * n:rows * n + rows]
             scores[h] = piece if scores[h] is None else scores[h] + piece
 
     lane = iota((rows, 128), 1)
@@ -337,22 +368,17 @@
         tops = jnp.where(head_of == h, top, tops)
         totals = jnp.where(head_of == h, jnp.sum(w, axis=1, keepdims=True), totals)
         weights.append(w.astype(BF16))
+    founds = [dot(jnp.concatenate(weights[3 * t:3 * t + 4], axis=0), value_parts[t].astype(BF16))
+              for t in range(5)]
     t1, t2, t3 = (x.astype(F32) for x in split3(tops))
     n1, n2, _ = (x.astype(F32) for x in split3(totals))
     stats = jnp.where(lane < 16, t1, jnp.where(lane < 32, t2, jnp.where(
         lane < 48, t3, jnp.where(lane < 64, n1, jnp.where(lane < 80, n2, 0.0)))))
 
-    w_v.wait()
     mixed = []
     for t in range(5):
-        value_t = dot(fb, wv[:, 256 * t:256 * t + 256]).astype(BF16)
-        found = dot(jnp.concatenate(weights[3 * t:3 * t + 4], axis=0), value_t)
-        total = None
-        for n, h in enumerate(range(3 * t, 3 * t + 4)):
-            low, high = D * h - 256 * t, D * h + D - 256 * t
-            piece = jnp.where((lane256 >= low) & (lane256 < high),
-                              found[rows * n:rows * n + rows], 0.0)
-            total = piece if total is None else total + piece
+        total = sum(jnp.where(inside(h, t), founds[t][rows * n:rows * n + rows], 0.0)
+                    for n, h in enumerate(heads_of(t)))
         mixed += [total[:, :128], total[:, 128:]]
     for d in range(COLS):
         block = [m[8 * d:8 * d + 8] for m in mixed + [stats]] + [jnp.zeros((8, 128), F32)]
@@ -411,10 +437,10 @@
             device_id=(2 * p + 1 - k, c), device_id_type=MESH)
 
     targets = (
+        (2 * p, c + 1, c <= 4),
+        (2 * p + 1, c - 3, c >= 3),
         (2 * p - 1, 5, (c == 0) & (p > 0)),
         (2 * p + 2, 0, (c == COLS - 1) & (p < ROWS // 2 - 1)),
-        (2 * p, c + 1, c <= 4),
-        (2 * p + 1, c - 3, c >= 3),
     )
     w_o.wait()
     w_pa.wait()
@@ -439,10 +465,7 @@
         factor = jnp.concatenate([s / whole for s in scales], axis=0)
         high = factor.astype(BF16).astype(F32)
         factor = jnp.where(b < H, high, jnp.where(b < 2 * H, factor - high, 0.0)).astype(BF16)
-        l, f = iota((128, E), 0), iota((128, E), 1)
-        first = (l & (H - 1)) * D
-        spread = jnp.where((l < 2 * H) & (f >= first) & (f < first + D), 1.0, 0.0).astype(BF16)
-        factors = dot(factor, spread)
+        factors = dot(factor, spread[...])
         attended = []
         for t in range(10):
             attended.append(sum(
@@ -470,7 +493,7 @@
                     def _():
                         pa_copy(row, col, slot, n).start()
 
-    fb_whole().wait_send()
+    fb_some(ROWS - 1, 0).wait_send()
     fa_whole().wait_send()
     fa_sibling().wait_send()
     sib_copy().wait_send()
@@ -684,6 +707,9 @@
             pltpu.VMEM((ROWS, D, HALF), BF16),
             pltpu.VMEM((2, COLS, TILE_A, E // COLS), BF16),
             pltpu.VMEM((2 * TILE_A, E), F32),
+            pltpu.VMEM((HALF, E), F32),
+            pltpu.VMEM((HALF, E), F32),
+            pltpu.VMEM((128, E), BF16),
             pltpu.VMEM((COLS, 96, 128), BF16),
             pltpu.VMEM((2 * COLS, 96, 128), BF16),
             pltpu.VMEM((HALF // 2, 128), F32),
@@ -695,7 +721,7 @@
             pltpu.VMEM((6, 8, 128), F32),
             pltpu.VMEM((2, 32, 128), F32),
             dma((12,)),
-            dma, dma,
+            dma, dma((2,)),
             dma((2,)), dma((2,)),
             dma, dma,
             dma((3,)), dma((3,)),

time: 38.8 us -> 37 us (0.954)
  Pallas kernels: 37.2 us -> 35.4 us
    pallas_call x1, Pallas kernels: 37.2 us -> 35.4 us  [local(): pl.pallas_call(attention, out_shape=jax.ShapeDtypeStruct((TILE_A, TILE_B)...]
where the time goes in v4:
time: 37 us; the launch traced here: 36.8 us
  Pallas kernels  35.4 us (96%)
  local copies, waits for them, and re-layouts  1.38 us (4%)
    pallas_call x1, Pallas kernels, local(): pl.pallas_call(attention, out_shape=jax.ShapeDtypeStruct((TILE_A, TILE_B)...  35.4 us
    unnamed x1, local copies, waits for them, and re-layouts  1.38 us

profile of v4, /device:TPU:1, one launch (start us, length us, event | category | flops | bytes accessed | tf_op | source)
XLA Modules:
  0.0 36.8 jit_solution(12521236442743553385)
XLA Ops:
  0.0 35.4 %contact_map.1 = f32[32,256]{1,0:T(8,128)} custom-call(bf16[32,160]{1,0:T(8,128)(2,1)} %ea_h.1, bf16[80,256]{1,0:T(8,128)(2,1)} %bitcast.7, bf16[1280,1280]{1,0:T(8,128)(2,1)} %wq_h.1, bf16[1280,1280]{1,0:T(8,128)(2,1)} %wk_h.1, bf16[1280,1280]{1,0:T(8,128)(2,1)} %wv_h.1, bf16[1280,1280]{1,0:T(8,128)(2,1)} %wo_h.1, bf16[64,1280]{1,0:T(8,128)(2,1)} %bitcast.5, ...), custom_call_target="tpu_custom_call" | custom-call | tf_op jit(solution)/shard_map/contact_map/pallas_call | solution.py:681
  35.5 1.4 %copy.13 = f32[32,256]{1,0:T(8,128)} copy(f32[32,256]{1,0:T(8,128)} %contact_map.1) | data formatting | bytes 65536

commit v5 on v4

--- a/solution.py
+++ b/solution.py
@@ -680,7 +680,7 @@
     dma = pltpu.SemaphoreType.DMA
     return pl.pallas_call(
         attention,
-        out_shape=jax.ShapeDtypeStruct((TILE_A, TILE_B), F32),
+        out_shape=pltpu.VMEM((TILE_A, TILE_B), F32),
         in_specs=[hbm] * 11,
         out_specs=vmem,
         scratch_shapes=[
@@ -728,10 +728,11 @@
             dma((4,)), dma((6,)),
         ],
         compiler_params=pltpu.CompilerParams(
-            collective_id=0, has_side_effects=True, vmem_limit_bytes=60 * 2 ** 20),
+            collective_id=0, has_side_effects=True, vmem_limit_bytes=48 * 2 ** 20),
         name="contact_map",
-    )(emb_a, emb_b.T, w_query, w_key, w_value, w_out, w_pair_a.T, w_pair_b.T,
-      jnp.transpose(w_depth, (2, 0, 1)), w_point, w_logit.reshape(1, C))
+    )(*(pltpu.with_memory_space_constraint(a, pltpu.HBM) for a in (
+        emb_a, emb_b.T, w_query, w_key, w_value, w_out, w_pair_a.T, w_pair_b.T,
+        jnp.transpose(w_depth, (2, 0, 1)), w_point, w_logit.reshape(1, C))))
 
 
 def solution(mesh):

time: 37 us -> 35.6 us (0.962)
  local copies, waits for them, and re-layouts: 1.38 us -> 0.62 us
  Pallas kernels: 35.4 us -> 34.8 us
    unnamed x1, local copies, waits for them, and re-layouts: 1.38 us -> 0.62 us
    pallas_call x1, Pallas kernels: 35.4 us -> 34.8 us  [local(): pl.pallas_call(attention, out_shape=pltpu.VMEM((TILE_A, TILE_B), F32), in...]
where the time goes in v5:
time: 35.6 us; the launch traced here: 35.5 us
  Pallas kernels  34.8 us (98%)
  local copies, waits for them, and re-layouts  0.62 us (2%)
    pallas_call x1, Pallas kernels, local(): pl.pallas_call(attention, out_shape=pltpu.VMEM((TILE_A, TILE_B), F32), in...  34.8 us

profile of v5, /device:TPU:1, one launch (start us, length us, event | category | flops | bytes accessed | tf_op | source)
XLA Modules:
  0.0 35.5 jit_solution(14854138434541856002)
XLA Ops:
  0.0 34.8 %contact_map.1 = f32[32,256]{1,0:T(8,128)S(1)} custom-call(bf16[32,160]{1,0:T(8,128)(2,1)} %ea_h.1, bf16[80,256]{1,0:T(8,128)(2,1)} %bitcast.7, bf16[1280,1280]{1,0:T(8,128)(2,1)} %wq_h.1, bf16[1280,1280]{1,0:T(8,128)(2,1)} %wk_h.1, bf16[1280,1280]{1,0:T(8,128)(2,1)} %wv_h.1, bf16[1280,1280]{1,0:T(8,128)(2,1)} %wo_h.1, bf16[64,1280]{1,0:T(8,128)(2,1)} %bitcast.5, ...), custom_call_target="tpu_custom_call" | custom-call | tf_op jit(solution)/shard_map/contact_map/pallas_call | solution.py:681
  34.9 0.6 %copy.13 = f32[32,256]{1,0:T(8,128)} copy(f32[32,256]{1,0:T(8,128)S(1)} %contact_map.1) | data formatting | bytes 65536

commit v6 on v5

--- a/solution.py
+++ b/solution.py
@@ -74,16 +74,15 @@
 
     for u in range(5):
         row_w[u:u + 1] = sum(tap(u, v) for v in range(5))
-    for n, start in enumerate((0, QW - 8)):
-        column = 2 * (iota((8, 128), 0) + start) + jnp.where(iota((8, 128), 1) < C, 0, 1)
-        column = column + TILE_B * c - 2
+    for n, start in enumerate((1, HALF)):
+        column = 2 * start + jnp.where(iota((1, 128), 1) < C, 0, 1) + TILE_B * c - 2
         for u in range(5):
             total = None
             for v in range(5):
                 at = column + (v - 2)
                 piece = jnp.where((at >= 0) & (at < LB), tap(u, v), 0.0)
                 total = piece if total is None else total + piece
-            edge_w[n, u] = total
+            edge_w[n, u:u + 1] = total
 
     a, b = iota((128, 128), 0), iota((128, 128), 1)
     upper, left = a < C, b < C
@@ -532,7 +531,7 @@
             pa_copy(r, c, s, 0).wait_recv()
 
         pa_buf[8 * s:8 * s + 8] = pa_land[s]
-    row_parts(pa_buf, row_w, edge_w, a_mid, a_edge, range(4, 32), r)
+    row_parts(pa_buf, row_w, edge_w, a_mid, a_edge, ((4, 32),), r)
     for _ in first(list(range(4, 32, 2))):
         pass
     part1 = second(1)
@@ -553,7 +552,7 @@
     def _():
         pa_buf[40:48] = pa_land[5]
 
-    row_parts(pa_buf, row_w, edge_w, a_mid, a_edge, (0, 1, 2, 3, 32, 33, 34, 35), r)
+    row_parts(pa_buf, row_w, edge_w, a_mid, a_edge, ((0, 4), (32, 36)), r)
     for _ in first([0, 2, 32, 34]):
         pass
     part0 = second(0)
@@ -575,24 +574,28 @@
 
 
 def gelu_twice(x):
-    inner = x * (0.7978845608028654 + 0.035677408136300125 * (x * x))
+    x = x.astype(BF16)
+    inner = x * (BF16(0.7978845608028654) + BF16(0.035677408136300125) * (x * x))
     return x + x * jnp.tanh(inner)
 
 
-def row_parts(pa_buf, row_w, edge_w, a_mid, a_edge, rows, r):
+def squared(x):
+    x = x.astype(BF16)
+    return x * x
+
+
+def row_parts(pa_buf, row_w, edge_w, a_mid, a_edge, spans, r):
     place = iota((48, 128), 0) + (TILE_A * r - 8)
     pa = jnp.where((place >= 0) & (place < LA), pa_buf[...], 0.0)
-    middle = sum(row_w[u:u + 1] * pa[4 + u:44 + u] for u in range(5))
-    weights = [[edge_w[n, u] for u in range(5)] for n in range(2)]
-    edges = [sum(weights[n][u] * pa[4 + u + i:5 + u + i] for u in range(5))
-             for n in range(2) for i in rows]
-    value = jnp.concatenate([middle] + edges, axis=0)
+    kinds = [[row_w[u:u + 1] for u in range(5)]]
+    kinds += [[edge_w[n, u:u + 1] for u in range(5)] for n in range(2)]
+    value = jnp.concatenate(
+        [sum(w[u] * pa[4 + u:44 + u] for u in range(5)) for w in kinds], axis=0)
     value = value - near_dot(value, mean_matrix(128))
-    for m, i in enumerate(rows):
-        a_mid[i:i + 1] = value[i:i + 1]
-        a_edge[0, 8 * i:8 * i + 8] = value[40 + 8 * m:48 + 8 * m]
-        at = 40 + 8 * (len(rows) + m)
-        a_edge[1, 8 * i:8 * i + 8] = value[at:at + 8]
+    for low, high in spans:
+        a_mid[low:high] = value[low:high]
+        a_edge[0, low:high] = value[40 + low:40 + high]
+        a_edge[1, low:high] = value[80 + low:80 + high]
 
 
 def first_blocks(rows, r, in_map, mean, pa_buf, pb_mid, b_part, a_mid, a_edge, point_w, f1):
@@ -600,19 +603,22 @@
     kinds = {2: jnp.where(top, 0, 2), 3: jnp.where(top, 1, 2),
              32: jnp.where(bottom, 3, 2), 33: jnp.where(bottom, 4, 2)}
 
+    sub = iota((8, 128), 0)
+
     def part_of(w):
         part = b_part[kinds.get(w, 2)]
+        row = a_mid[w:w + 1]
         return jnp.concatenate([
-            part[:8] + a_edge[0, 8 * w:8 * w + 8],
-            part[8:128] + a_mid[w:w + 1],
-            part[128:] + a_edge[1, 8 * w:8 * w + 8]], axis=0)
+            part[:8] + jnp.where(sub == 1, a_edge[0, w:w + 1], row),
+            part[8:HALF] + row,
+            part[HALF:] + jnp.where(sub == 0, a_edge[1, w:w + 1], row)], axis=0)
 
     def start(u):
         x = jnp.concatenate([part_of(u), part_of(u + 1)], axis=1)
-        return x, dot((x * x).astype(BF16), mean)
+        return x, dot(squared(x), mean)
 
     def middle(x, var):
-        return dot(gelu_twice(x * lax.rsqrt(var + 1e-5)).astype(BF16), point_w[...])
+        return dot(gelu_twice(x * lax.rsqrt(var + 1e-5)), point_w[...])
 
     def end(u, update):
         for n in range(2):
@@ -650,8 +656,8 @@
 
 
 def read_out(step, x, field, mean, head_w, logits):
-    var = dot((x * x).astype(BF16), mean)
-    g = gelu_twice(x * lax.rsqrt(var + 1e-5)).astype(BF16)
+    var = dot(squared(x), mean)
+    g = gelu_twice(x * lax.rsqrt(var + 1e-5))
     found = dot(head_w[...], jnp.concatenate(field + [g], axis=1), NT)
     found = found[0:4] + found[4:8]
     for n in range(4):
@@ -688,12 +694,12 @@
             pltpu.VMEM((QW, 128), F32),
             pltpu.VMEM((5, QW, 128), F32),
             pltpu.VMEM((8, 128), F32),
-            pltpu.VMEM((2, 5, 8, 128), F32),
+            pltpu.VMEM((2, 8, 128), F32),
             pltpu.VMEM((18 * 128, 256), BF16),
             pltpu.VMEM((256, 256), BF16),
             pltpu.VMEM((8, 512), BF16),
             pltpu.VMEM((40, 128), F32),
-            pltpu.VMEM((2, 288, 128), F32),
+            pltpu.VMEM((2, 40, 128), F32),
             pltpu.VMEM((36, QW, 128), F32),
             pltpu.VMEM((2 * TILE_A, 128), F32),
             pltpu.VMEM((TILE_A, E // COLS), BF16),

time: 35.6 us -> 34.7 us (0.975)
  Pallas kernels: 34.8 us -> 34 us
    pallas_call x1, Pallas kernels: 34.8 us -> 34 us  [local(): pl.pallas_call(attention, out_shape=pltpu.VMEM((TILE_A, TILE_B), F32), in...]
where the time goes in v6:
time: 34.7 us; the launch traced here: 34.6 us
  Pallas kernels  34 us (98%)
  local copies, waits for them, and re-layouts  0.62 us (2%)
    pallas_call x1, Pallas kernels, local(): pl.pallas_call(attention, out_shape=pltpu.VMEM((TILE_A, TILE_B), F32), in...  34 us

profile of v6, /device:TPU:1, one launch (start us, length us, event | category | flops | bytes accessed | tf_op | source)
XLA Modules:
  0.0 34.6 jit_solution(8137192054613792285)
XLA Ops:
  0.0 34.0 %contact_map.1 = f32[32,256]{1,0:T(8,128)S(1)} custom-call(bf16[32,160]{1,0:T(8,128)(2,1)} %ea_h.1, bf16[80,256]{1,0:T(8,128)(2,1)} %bitcast.7, bf16[1280,1280]{1,0:T(8,128)(2,1)} %wq_h.1, bf16[1280,1280]{1,0:T(8,128)(2,1)} %wk_h.1, bf16[1280,1280]{1,0:T(8,128)(2,1)} %wv_h.1, bf16[1280,1280]{1,0:T(8,128)(2,1)} %wo_h.1, bf16[64,1280]{1,0:T(8,128)(2,1)} %bitcast.5, ...), custom_call_target="tpu_custom_call" | custom-call | tf_op jit(solution)/shard_map/contact_map/pallas_call | solution.py:687
  34.0 0.6 %copy.13 = f32[32,256]{1,0:T(8,128)} copy(f32[32,256]{1,0:T(8,128)S(1)} %contact_map.1) | data formatting | bytes 65536

commit v7 on v6

--- a/solution.py
+++ b/solution.py
@@ -166,13 +166,13 @@
         pltpu.make_async_copy(src, dst, in_sem.at[i])
         for i, (src, dst) in enumerate(
             [(eb_h.at[:, pl.ds(0, HALF)], fb_src.at[0]), (eb_h.at[:, pl.ds(HALF, HALF)], fb_src.at[1]),
-             (ea_h, ea), (wq_h, wq), (wk_h, wk), (wv_h, wv),
-             (wpb_h, wpb), (wo_h, wo), (wpa_h, wpa), (wd_h, wd), (wp_h, wp), (wl_h, wl)]
+             (ea_h, ea), (wd_h, wd), (wp_h, wp), (wl_h, wl), (wk_h, wk), (wv_h, wv),
+             (wpb_h, wpb), (wq_h, wq), (wo_h, wo), (wpa_h, wpa)]
         )
     ]
-    for load in loads:
+    for load in loads[:3]:
         load.start()
-    w_eb0, w_eb1, w_ea, w_q, w_k, w_v, w_pb, w_o, w_pa, w_d, w_p, w_l = loads
+    w_eb0, w_eb1, w_ea, w_d, w_p, w_l, w_k, w_v, w_pb, w_q, w_o, w_pa = loads
 
     x, y = lax.div(r, 8), lax.rem(p, 4)
     z, xl = lax.div(c, 2), lax.rem(c, 2)
@@ -202,6 +202,9 @@
     @pl.when((k == 0) & (r > 0))
     def _():
         greet(r - 2, COLS - 1)
+
+    for load in loads[3:]:
+        load.start()
 
     w_eb0.wait()
     w_eb1.wait()
@@ -300,40 +303,6 @@
 
     fb_some(8, 1).wait_recv()
     far = features(1 - x)
-    found_b = near_b + dot(far, pair_weights(1 - x), NT)
-    pb_own[...] = jnp.where(iota((HALF // 2, 128), 1) < C, found_b[:HALF // 2], found_b[HALF // 2:])
-
-    def sib_copy():
-        return pltpu.make_async_remote_copy(
-            src_ref=pb_own, dst_ref=pb_sib, send_sem=pb_s.at[0], recv_sem=pb_r.at[0],
-            device_id=(2 * p + 1 - k, c), device_id_type=MESH)
-
-    def right_copy(kk):
-        return pltpu.make_async_remote_copy(
-            src_ref=pb_own.at[pl.ds(HALF // 2 - 8, 8)], dst_ref=pb_left,
-            send_sem=pb_s.at[1 + kk], recv_sem=pb_r.at[1],
-            device_id=(2 * p + kk, lax.rem(c + 1, COLS)), device_id_type=MESH)
-
-    def left_copy(kk):
-        return pltpu.make_async_remote_copy(
-            src_ref=pb_own.at[pl.ds(0, 8)], dst_ref=pb_right,
-            send_sem=pb_s.at[1 + kk], recv_sem=pb_r.at[2],
-            device_id=(2 * p + kk, lax.rem(c + COLS - 1, COLS)), device_id_type=MESH)
-
-    sends_right = (k == 1) & (c < COLS - 1)
-    sends_left = (k == 0) & (c > 0)
-    sib_copy().start()
-
-    @pl.when(sends_right)
-    def _():
-        right_copy(0).start()
-        right_copy(1).start()
-
-    @pl.when(sends_left)
-    def _():
-        left_copy(0).start()
-        left_copy(1).start()
-
     rows = 2 * TILE_A
     lane256 = iota((rows, 256), 1)
 
@@ -403,6 +372,40 @@
     def _():
         rs_copy(0).start()
 
+    found_b = near_b + dot(far, pair_weights(1 - x), NT)
+    pb_own[...] = jnp.where(iota((HALF // 2, 128), 1) < C, found_b[:HALF // 2], found_b[HALF // 2:])
+
+    def sib_copy():
+        return pltpu.make_async_remote_copy(
+            src_ref=pb_own, dst_ref=pb_sib, send_sem=pb_s.at[0], recv_sem=pb_r.at[0],
+            device_id=(2 * p + 1 - k, c), device_id_type=MESH)
+
+    def right_copy(kk):
+        return pltpu.make_async_remote_copy(
+            src_ref=pb_own.at[pl.ds(HALF // 2 - 8, 8)], dst_ref=pb_left,
+            send_sem=pb_s.at[1 + kk], recv_sem=pb_r.at[1],
+            device_id=(2 * p + kk, lax.rem(c + 1, COLS)), device_id_type=MESH)
+
+    def left_copy(kk):
+        return pltpu.make_async_remote_copy(
+            src_ref=pb_own.at[pl.ds(0, 8)], dst_ref=pb_right,
+            send_sem=pb_s.at[1 + kk], recv_sem=pb_r.at[2],
+            device_id=(2 * p + kk, lax.rem(c + COLS - 1, COLS)), device_id_type=MESH)
+
+    sends_right = (k == 1) & (c < COLS - 1)
+    sends_left = (k == 0) & (c > 0)
+    sib_copy().start()
+
+    @pl.when(sends_right)
+    def _():
+        right_copy(0).start()
+        right_copy(1).start()
+
+    @pl.when(sends_left)
+    def _():
+        left_copy(0).start()
+        left_copy(1).start()
+
     sib_copy().wait_recv()
 
     @pl.when(c > 0)
@@ -455,8 +458,8 @@
         same = (a & (H - 1)) == (b & (H - 1))
         pick_top = jnp.where(same & (a < 48), 1.0, 0.0).astype(BF16)
         pick_total = jnp.where(same & (a >= 48) & (a < 80), 1.0, 0.0).astype(BF16)
-        top = dot(stat, pick_top)
-        total = dot(stat, pick_total)
+        picked = dot(stat, jnp.concatenate([pick_top, pick_total], axis=1))
+        top, total = picked[:, :128], picked[:, 128:]
         tops = [top[8 * g:8 * g + 8] for g in range(2 * COLS)]
         summit = functools.reduce(jnp.maximum, tops)
         scales = [jnp.exp(x - summit) for x in tops]

time: 34.7 us -> 34.4 us (level)
  no operation moved by 1% of the time
where the time goes in v7:
time: 34.4 us; the launch traced here: 34.3 us
  Pallas kernels  33.7 us (98%)
  local copies, waits for them, and re-layouts  0.62 us (2%)
    pallas_call x1, Pallas kernels, local(): pl.pallas_call(attention, out_shape=pltpu.VMEM((TILE_A, TILE_B), F32), in...  33.7 us

profile of v7, /device:TPU:1, one launch (start us, length us, event | category | flops | bytes accessed | tf_op | source)
XLA Modules:
  0.0 34.3 jit_solution(4944569165769159948)
XLA Ops:
  0.0 33.7 %contact_map.1 = f32[32,256]{1,0:T(8,128)S(1)} custom-call(bf16[32,160]{1,0:T(8,128)(2,1)} %ea_h.1, bf16[80,256]{1,0:T(8,128)(2,1)} %bitcast.7, bf16[1280,1280]{1,0:T(8,128)(2,1)} %wq_h.1, bf16[1280,1280]{1,0:T(8,128)(2,1)} %wk_h.1, bf16[1280,1280]{1,0:T(8,128)(2,1)} %wv_h.1, bf16[1280,1280]{1,0:T(8,128)(2,1)} %wo_h.1, bf16[64,1280]{1,0:T(8,128)(2,1)} %bitcast.5, ...), custom_call_target="tpu_custom_call" | custom-call | tf_op jit(solution)/shard_map/contact_map/pallas_call | solution.py:690
  33.7 0.6 %copy.13 = f32[32,256]{1,0:T(8,128)} copy(f32[32,256]{1,0:T(8,128)S(1)} %contact_map.1) | data formatting | bytes 65536

commit v8 on v7

--- a/solution.py
+++ b/solution.py
@@ -152,7 +152,7 @@
     out_ref,
     pa_buf, pb_mid, b_part, row_w, edge_w, conv_w, point_w, head_w, a_mid, a_edge, f1, logits,
     ea, wq, wk, wv, wo, wpa, wpb, wd, wp, wl,
-    fb_src, fb_all, fa_all, fa_rows, keys, values, spread, msg, land,
+    fb_src, fb_all, fa_all, fa_rows, keys, values, masked, spread, msg, land,
     pb_own, pb_sib, pb_left, pb_right, pb_buf, pa_own, pa_land, taps,
     in_sem, fb_s, fb_r, fa_s, fa_r, rs_s, rs_r, pb_s, pb_r, pa_s, pa_r,
 ):
@@ -301,20 +301,22 @@
     w_q.wait()
     query = dot(fa.astype(BF16), wq[...]).astype(BF16).astype(F32)
 
+    rows = 2 * TILE_A
+    lane256 = iota((rows, 256), 1)
+
+    def heads_of(t):
+        return range(3 * t, 3 * t + 4)
+
+    def inside(h, t):
+        return (lane256 >= D * h - 256 * t) & (lane256 < D * h + D - 256 * t)
+
+    spans = [slice(256 * t, 256 * t + 256) for t in range(5)]
+    for t in range(5):
+        masked[t] = jnp.concatenate([jnp.where(inside(h, t), query[:, spans[t]], 0.0)
+                                     for h in heads_of(t)], axis=0).astype(BF16)
+
     fb_some(8, 1).wait_recv()
     far = features(1 - x)
-    rows = 2 * TILE_A
-    lane256 = iota((rows, 256), 1)
-
-    def heads_of(t):
-        return range(3 * t, 3 * t + 4)
-
-    def inside(h, t):
-        return (lane256 >= D * h - 256 * t) & (lane256 < D * h + D - 256 * t)
-
-    spans = [slice(256 * t, 256 * t + 256) for t in range(5)]
-    masked = [jnp.concatenate([jnp.where(inside(h, t), query[:, spans[t]], 0.0)
-                               for h in heads_of(t)], axis=0).astype(BF16) for t in range(5)]
     key_parts = [keys[:, at] + dot(far, wk[some_rows(1 - x), at]) for at in spans]
     founds = [dot(masked[t], key_parts[t].astype(BF16), NT) for t in range(5)]
     value_parts = [values[:, at] + dot(far, wv[some_rows(1 - x), at]) for at in spans]
@@ -718,6 +720,7 @@
             pltpu.VMEM((2 * TILE_A, E), F32),
             pltpu.VMEM((HALF, E), F32),
             pltpu.VMEM((HALF, E), F32),
+            pltpu.VMEM((5, 8 * TILE_A, 256), BF16),
             pltpu.VMEM((128, E), BF16),
             pltpu.VMEM((COLS, 96, 128), BF16),
             pltpu.VMEM((2 * COLS, 96, 128), BF16),

time: 34.4 us -> 34.4 us (level)
  no operation moved by 1% of the time
where the time goes in v8:
time: 34.4 us; the launch traced here: 34.3 us
  Pallas kernels  33.7 us (98%)
  local copies, waits for them, and re-layouts  0.62 us (2%)
    pallas_call x1, Pallas kernels, local(): pl.pallas_call(attention, out_shape=pltpu.VMEM((TILE_A, TILE_B), F32), in...  33.7 us

profile of v8, /device:TPU:1, one launch (start us, length us, event | category | flops | bytes accessed | tf_op | source)
XLA Modules:
  0.0 34.3 jit_solution(16204494468377421792)
XLA Ops:
  0.0 33.7 %contact_map.1 = f32[32,256]{1,0:T(8,128)S(1)} custom-call(bf16[32,160]{1,0:T(8,128)(2,1)} %ea_h.1, bf16[80,256]{1,0:T(8,128)(2,1)} %bitcast.7, bf16[1280,1280]{1,0:T(8,128)(2,1)} %wq_h.1, bf16[1280,1280]{1,0:T(8,128)(2,1)} %wk_h.1, bf16[1280,1280]{1,0:T(8,128)(2,1)} %wv_h.1, bf16[1280,1280]{1,0:T(8,128)(2,1)} %wo_h.1, bf16[64,1280]{1,0:T(8,128)(2,1)} %bitcast.5, ...), custom_call_target="tpu_custom_call" | custom-call | tf_op jit(solution)/shard_map/contact_map/pallas_call | solution.py:692
  33.7 0.6 %copy.13 = f32[32,256]{1,0:T(8,128)} copy(f32[32,256]{1,0:T(8,128)S(1)} %contact_map.1) | data formatting | bytes 65536

commit v9 on v8

--- a/solution.py
+++ b/solution.py
@@ -152,7 +152,7 @@
     out_ref,
     pa_buf, pb_mid, b_part, row_w, edge_w, conv_w, point_w, head_w, a_mid, a_edge, f1, logits,
     ea, wq, wk, wv, wo, wpa, wpb, wd, wp, wl,
-    fb_src, fb_all, fa_all, fa_rows, keys, values, masked, spread, msg, land,
+    fb_src, fb_all, fa_all, fa_rows, keys, values, masked, spread, pick, wpa2, msg, land,
     pb_own, pb_sib, pb_left, pb_right, pb_buf, pa_own, pa_land, taps,
     in_sem, fb_s, fb_r, fa_s, fa_r, rs_s, rs_r, pb_s, pb_r, pa_s, pa_r,
 ):
@@ -448,6 +448,11 @@
     )
     w_o.wait()
     w_pa.wait()
+    wpa2[0:C] = wpa[...]
+    wpa2[C:2 * C] = wpa[...]
+    l, f = iota((128, 256), 0), iota((128, 256), 1)
+    wanted = (((f < 128) & (l < 48)) | ((f >= 128) & (l >= 48) & (l < 80))) & ((l & (H - 1)) == (f & (H - 1)))
+    pick[...] = jnp.where(wanted, 1.0, 0.0).astype(BF16)
 
     @pl.when(k == 0)
     def _():
@@ -456,11 +461,8 @@
         rs_whole(2 * COLS - 1).wait_recv()
         got = [land[g].astype(F32) for g in range(2 * COLS)]
         stat = jnp.concatenate([x[80:88] for x in got], axis=0).astype(BF16)
-        a, b = iota((128, 128), 0), iota((128, 128), 1)
-        same = (a & (H - 1)) == (b & (H - 1))
-        pick_top = jnp.where(same & (a < 48), 1.0, 0.0).astype(BF16)
-        pick_total = jnp.where(same & (a >= 48) & (a < 80), 1.0, 0.0).astype(BF16)
-        picked = dot(stat, jnp.concatenate([pick_top, pick_total], axis=1))
+        b = iota((128, 128), 1)
+        picked = dot(stat, pick[...])
         top, total = picked[:, :128], picked[:, 128:]
         tops = [top[8 * g:8 * g + 8] for g in range(2 * COLS)]
         summit = functools.reduce(jnp.maximum, tops)
@@ -480,7 +482,7 @@
         centre = hidden - jnp.mean(hidden, axis=1, keepdims=True)
         spread_h = jnp.mean(centre * centre, axis=1, keepdims=True)
         normed = (centre * lax.rsqrt(spread_h + 1e-5)).astype(BF16)
-        pa_own[...] = dot(normed, jnp.concatenate([wpa[...], wpa[...]], axis=0), NT)
+        pa_own[...] = dot(normed, wpa2[...], NT)
         for n, (row, slot, on) in enumerate(targets):
             @pl.when(on)
             def _():
@@ -722,6 +724,8 @@
             pltpu.VMEM((HALF, E), F32),
             pltpu.VMEM((5, 8 * TILE_A, 256), BF16),
             pltpu.VMEM((128, E), BF16),
+            pltpu.VMEM((128, 256), BF16),
+            pltpu.VMEM((2 * C, E), BF16),
             pltpu.VMEM((COLS, 96, 128), BF16),
             pltpu.VMEM((2 * COLS, 96, 128), BF16),
             pltpu.VMEM((HALF // 2, 128), F32),

time: 34.4 us -> 34.5 us (level)
  no operation moved by 1% of the time
where the time goes in v9:
time: 34.5 us; the launch traced here: 34.3 us
  Pallas kernels  33.7 us (98%)
  local copies, waits for them, and re-layouts  0.62 us (2%)
    pallas_call x1, Pallas kernels, local(): pl.pallas_call(attention, out_shape=pltpu.VMEM((TILE_A, TILE_B), F32), in...  33.7 us

profile of v9, /device:TPU:1, one launch (start us, length us, event | category | flops | bytes accessed | tf_op | source)
XLA Modules:
  0.0 34.3 jit_solution(1434472912419977082)
XLA Ops:
  0.0 33.7 %contact_map.1 = f32[32,256]{1,0:T(8,128)S(1)} custom-call(bf16[32,160]{1,0:T(8,128)(2,1)} %ea_h.1, bf16[80,256]{1,0:T(8,128)(2,1)} %bitcast.7, bf16[1280,1280]{1,0:T(8,128)(2,1)} %wq_h.1, bf16[1280,1280]{1,0:T(8,128)(2,1)} %wk_h.1, bf16[1280,1280]{1,0:T(8,128)(2,1)} %wv_h.1, bf16[1280,1280]{1,0:T(8,128)(2,1)} %wo_h.1, bf16[64,1280]{1,0:T(8,128)(2,1)} %bitcast.5, ...), custom_call_target="tpu_custom_call" | custom-call | tf_op jit(solution)/shard_map/contact_map/pallas_call | solution.py:694
  33.7 0.6 %copy.13 = f32[32,256]{1,0:T(8,128)} copy(f32[32,256]{1,0:T(8,128)S(1)} %contact_map.1) | data formatting | bytes 65536
